TPU v7x, 32 devices: a whole 2x2x4 slice. The times are simulated.
32 devices in a mesh: pipe: 4 (over y, x), dp: 8 (over z, core).
Axes of the slice: x: 2, y: 2, z: 4, core: 2. Of those that a mesh axis runs over, the one named last changes fastest.
Arguments:
- clips: bfloat16 [2, 3, 1024, 1536], P(None, None, 'dp'), may hold values from -6 to 6
- positions: int32 [3, 2, 3, 1024], P(None, None, None, 'dp'), may hold values from 0 to 79, as said below
- out_proj: bfloat16 [4, 1536, 1536], P('pipe', 'dp'), may hold values from -0.15625 to 0.15625
- qk_gains: bfloat16 [4, 2, 128], P('pipe'), may hold values from -1.5 to 1.5
- cotangent: bfloat16 [2, 3, 1024, 1536], P(None, None, 'dp'), may hold values from -0.1875 to 0.1875
Outputs:
- grad_out_proj: float32 [4, 1536, 1536], P('pipe', 'dp')
- grad_gains: float32 [4, 2, 128], P('pipe')
Inputs may be any that keep to these rules, and one draw needn't show every extreme that they name: positions[0] is a token's frame, positions[1] its row and positions[2] its column in the latent video.
All inputs are finite; a program needn't handle non-finite values.
Results may differ from a plain program's by a relative error of at most 0.018.
Values may be sent and summed in bfloat16 or wider, within the bound.
No kernel may reach another device: no remote copies, remote signals or barrier semaphores. Data moves between devices by JAX's collectives and lax.ppermute only.
A program may use at most 192 MiB of HBM per device.

v0:
```python
import math

import jax
import jax.numpy as jnp
from jax import lax
from jax.sharding import PartitionSpec as P


def from_partner(x, axis, distance):
    return lax.ppermute(x, axis, [(i, i ^ 1 << distance) for i in range(lax.axis_size(axis))])


def shifted(block, axis, distance):
    devices = range(lax.axis_size(axis))
    route = [(i - distance, i) for i in devices if i - distance in devices]
    return lax.ppermute(block, axis, route)


def rotate(values, coords):
    head_size = values.shape[-1]
    first_width = head_size // 8
    rest_width = (head_size - first_width) // 2
    widths = (first_width, rest_width, rest_width)
    pieces = []
    offset = 0
    for axis_index in range(3):
        section = widths[axis_index]
        half_width = section // 2
        segment = values[..., offset : offset + section]
        frequency = 256.0 ** (-2.0 * jnp.arange(half_width, dtype=jnp.float32) / section)
        angles = coords[axis_index].astype(jnp.float32)[:, None] * frequency[None, :]
        cosine = jnp.cos(angles)[:, None, :]
        sine_part = jnp.sin(angles)[:, None, :]
        lower_half = segment[..., :half_width]
        upper_half = segment[..., half_width:]
        pieces.append(lower_half * cosine - upper_half * sine_part)
        pieces.append(lower_half * sine_part + upper_half * cosine)
        offset = offset + section
    return jnp.concatenate(pieces, axis=-1)


def mixing(hidden, gain_pair, coords):
    row_count, channels = hidden.shape
    head_size = gain_pair.shape[-1]
    by_heads = hidden.reshape(row_count, channels // head_size, head_size)
    wide_heads = by_heads.astype(jnp.float32)
    normed = wide_heads * lax.rsqrt(
        jnp.mean(wide_heads * wide_heads, axis=-1, keepdims=True) + 1e-06
    )
    queries = rotate(normed * gain_pair[0], coords)
    key_rows = rotate(normed * gain_pair[1], coords)
    scores = jnp.einsum(
        "qhe,khe->hqk", queries, key_rows, precision=lax.Precision.HIGHEST
    ) / math.sqrt(head_size)
    exp_scores = jnp.exp(scores)
    weights = (exp_scores / jnp.sum(exp_scores, axis=-1, keepdims=True)).astype(jnp.bfloat16)
    weights_wide = lax.optimization_barrier(weights).astype(jnp.float32)
    mixed_rows = jnp.einsum("hqk,khe->qhe", weights_wide, wide_heads)
    return mixed_rows.reshape(row_count, channels).astype(jnp.bfloat16)


def phase_forward(hidden, gain_pair, coords, weight):
    mixed_rows = mixing(hidden, gain_pair, coords)
    update = jnp.dot(mixed_rows, weight, preferred_element_type=jnp.float32)
    return (hidden.astype(jnp.float32) + update).astype(jnp.bfloat16)


def phase_backward(hidden, gain_pair, coords, weight, grad_out):

    def local_mix(state_rows, gain_values):
        return mixing(state_rows, gain_values, coords)

    mixed_rows, pullback = jax.vjp(local_mix, hidden, gain_pair)
    weight_term = lax.dot_general(
        mixed_rows, grad_out, (((0,), (0,)), ((), ())), preferred_element_type=jnp.float32
    )
    grad_mixed = lax.dot_general(
        grad_out, weight, (((1,), (1,)), ((), ())), preferred_element_type=jnp.float32
    ).astype(jnp.bfloat16)
    grad_hidden, gain_term = pullback(grad_mixed)
    grad_in = (grad_out.astype(jnp.float32) + grad_hidden.astype(jnp.float32)).astype(jnp.bfloat16)
    return (grad_in, weight_term, gain_term)


def shards(clips, positions, out_proj, qk_gains, cotangent):
    depth = lax.axis_size("pipe")
    place = lax.axis_index("pipe")
    mirror = depth - 1 - place
    micro_count = clips.shape[1]
    bit_count = depth.bit_length() - 1
    far_weight = out_proj[0]
    far_gains = qk_gains[0]
    for bit_index in range(bit_count):
        far_weight, far_gains = from_partner((far_weight, far_gains), "pipe", bit_index)
    near_full, far_full = (
        lax.all_gather(out_proj[0], "dp", axis=0, tiled=True),
        lax.all_gather(far_weight, "dp", axis=0, tiled=True),
    )
    near_pair = qk_gains[0].astype(jnp.float32)
    far_pair = far_gains.astype(jnp.float32)
    tick_count = depth + micro_count - 1
    zero_rows = jnp.zeros(clips.shape[2:], jnp.bfloat16)

    def slot_state(slot_value):
        live_slot = (slot_value >= 0) & (slot_value < micro_count)
        return (live_slot, jnp.clip(slot_value, 0, micro_count - 1))

    def forward_inputs(tick_index, carry):
        received_near, received_far, store_near, store_far = carry
        live_near, clip_near = slot_state(tick_index - place)
        live_far, clip_far = slot_state(tick_index - mirror)
        input_near = jnp.where(place == 0, clips[0, clip_near], received_near)
        input_far = jnp.where(place == depth - 1, clips[1, clip_far], received_far)
        store_near = store_near.at[clip_near].set(
            jnp.where(live_near, input_near, store_near[clip_near])
        )
        store_far = store_far.at[clip_far].set(jnp.where(live_far, input_far, store_far[clip_far]))
        return (
            (live_near, clip_near, input_near),
            (live_far, clip_far, input_far),
            store_near,
            store_far,
        )

    def forward_tick(carry, tick_index):
        near_info, far_info, store_near, store_far = forward_inputs(tick_index, carry)
        live_near, clip_near, input_near = near_info
        live_far, clip_far, input_far = far_info
        output_near = lax.cond(
            live_near,
            lambda: phase_forward(input_near, near_pair, positions[:, 0, clip_near], near_full),
            lambda: zero_rows,
        )
        output_far = lax.cond(
            live_far,
            lambda: phase_forward(input_far, far_pair, positions[:, 1, clip_far], far_full),
            lambda: zero_rows,
        )
        next_near = shifted(output_near, "pipe", 1)
        next_far = shifted(output_far, "pipe", -1)
        return ((next_near, next_far, store_near, store_far), None)

    empty_store = jnp.zeros((micro_count,) + clips.shape[2:], jnp.bfloat16)
    carry, unused = lax.scan(
        forward_tick, (zero_rows, zero_rows, empty_store, empty_store), jnp.arange(tick_count - 1)
    )
    unused_near, unused_far, store_near, store_far = forward_inputs(tick_count - 1, carry)

    def backward_phase(tick_index, carry):
        received_near, received_far, sum_near, sum_far, gain_near, gain_far = carry
        live_near, clip_near = slot_state(tick_index - mirror)
        live_far, clip_far = slot_state(tick_index - place)
        incoming_near = jnp.where(place == depth - 1, cotangent[0, clip_near], received_near)
        incoming_far = jnp.where(place == 0, cotangent[1, clip_far], received_far)

        def work_near():
            grad_in, weight_term, gain_term = phase_backward(
                store_near[clip_near],
                near_pair,
                positions[:, 0, clip_near],
                near_full,
                incoming_near,
            )
            return (grad_in, sum_near + weight_term, gain_near + gain_term)

        def skip_near():
            return (zero_rows, sum_near, gain_near)

        def work_far():
            grad_in, weight_term, gain_term = phase_backward(
                store_far[clip_far], far_pair, positions[:, 1, clip_far], far_full, incoming_far
            )
            return (grad_in, sum_far + weight_term, gain_far + gain_term)

        def skip_far():
            return (zero_rows, sum_far, gain_far)

        grad_near, sum_near, gain_near = lax.cond(live_near, work_near, skip_near)
        grad_far, sum_far, gain_far = lax.cond(live_far, work_far, skip_far)
        return (grad_near, grad_far, sum_near, sum_far, gain_near, gain_far)

    def backward_tick(carry, tick_index):
        grad_near, grad_far, sum_near, sum_far, gain_near, gain_far = backward_phase(
            tick_index, carry
        )
        next_near = shifted(grad_near, "pipe", -1)
        next_far = shifted(grad_far, "pipe", 1)
        return ((next_near, next_far, sum_near, sum_far, gain_near, gain_far), None)

    channels = clips.shape[3]
    zero_square = jnp.zeros((channels, channels), jnp.float32)
    zero_gains = jnp.zeros(near_pair.shape, jnp.float32)
    start_carry = (zero_rows, zero_rows, zero_square, zero_square, zero_gains, zero_gains)
    carry, unused = lax.scan(backward_tick, start_carry, jnp.arange(tick_count - 1))
    unused_near, unused_far, sum_near, sum_far, gain_near, gain_far = backward_phase(
        tick_count - 1, carry
    )
    near_shard, far_shard = (
        lax.psum_scatter(
            sum_near.astype(jnp.bfloat16), "dp", scatter_dimension=0, tiled=True
        ).astype(jnp.float32),
        lax.psum_scatter(
            sum_far.astype(jnp.bfloat16), "dp", scatter_dimension=0, tiled=True
        ).astype(jnp.float32),
    )
    near_gain_sum, far_gain_sum = lax.psum((gain_near, gain_far), "dp")
    for bit_index in range(bit_count):
        far_shard, far_gain_sum = (
            from_partner(far_shard.astype(jnp.bfloat16), "pipe", bit_index).astype(far_shard.dtype),
            from_partner(far_gain_sum.astype(jnp.bfloat16), "pipe", bit_index).astype(
                far_gain_sum.dtype
            ),
        )
    shard_total = near_shard + far_shard
    gains_total = near_gain_sum + far_gain_sum
    return (shard_total[None], gains_total[None])


def solution(mesh):
    placed = (
        P(None, None, "dp", None),
        P(None, None, None, "dp"),
        P("pipe", "dp", None),
        P("pipe", None, None),
        P(None, None, "dp", None),
    )
    return jax.shard_map(
        shards,
        mesh=mesh,
        in_specs=placed,
        out_specs=(P("pipe", "dp", None), P("pipe", None, None)),
        check_vma=False,
    )
```

profile of v0, /device:TPU:0, one launch (start us, length us, event | category | flops | bytes accessed | tf_op | source)
XLA Modules:
  0.0 1172.1 jit_solution(7270855462855204608)
XLA Ops:
  11.0 13.5 %collective-permute-done.6 = bf16[192,1536]{1,0:T(8,128)(2,1)S(1)} collective-permute-done((bf16[192,1536]{1,0:T(8,128)(2,1)}, bf16[192,1536]{1,0:T(8,128)(2,1)S(1)}, u32[]{:S(2)}, u32[]{:S(2)}) %collective-permute-start.6) | collective-permute-done | bytes 589856 | tf_op jit(solution)/shard_map/ppermute | solution.py:10
  26.3 12.9 %collective-permute-done.7 = bf16[192,1536]{1,0:T(8,128)(2,1)S(1)} collective-permute-done((bf16[192,1536]{1,0:T(8,128)(2,1)S(1)}, bf16[192,1536]{1,0:T(8,128)(2,1)S(1)}, u32[]{:S(2)}, u32[]{:S(2)}) %collective-permute-start.7) | collective-permute-done | bytes 589856 | tf_op jit(solution)/shard_map/ppermute | solution.py:10
  53.2 10.9 all-gather.6.cloned.1.call-done
  64.1 52.8 %all-gather.4.cloned.1.call-done = bf16[1536,1536]{1,0:T(8,128)(2,1)} async-done(((bf16[192,1536]{1,0:T(8,128)(2,1)}), bf16[1536,1536]{1,0:T(8,128)(2,1)}) %all-gather.4.cloned.1.call-update) | async-done | bytes 4718608 | tf_op jit(solution)/shard_map/all_gather | solution.py:97
  120.0 307.0 %while.42 = (s32[]{:T(128)}, bf16[128,1536]{1,0:T(8,128)(2,1)S(1)}, bf16[128,1536]{1,0:T(8,128)(2,1)}, bf16[3,128,1536]{1,2,0:T(8,128)(2,1)}, bf16[3,128,1536]{1...) while((s32[]{:T(128)}, bf16[128,1536]{1,0:T(8,128)(2,1)S(1)}, ...), condition=%wide.region_11.12_spmd, body=%wide.region_0.11_spmd.sunk | while | flops 1921670144 | bytes 62277136 | solution.py:144
  131.1 28.7 %conditional.12 = (bf16[128,1536]{1,0:T(8,128)(2,1)}) conditional(s32[]{:T(128)} %convert_element_type.768, () %tuple.355, (bf16[128,1536]{1,0:T(8,128)(2,1)S(1)}, f32[2,128]{1,0:T(2,128)}, s32[]{:T(128)}, s32[3,2,3,128]{3,2,1,0:T(4,128)}, bf16[1536,1536]{1,0:T(8,128)(2,1)}) %tuple.356), branch_computations={%region_1.1_spmd, %region_2.4_spmd} | conditional | flops 960245248 | bytes 24682602 | solution.py:129
  141.5 4.4 concatenate.50
  164.4 6.0 collective-permute-done
  181.4 28.7 %conditional.12 = (bf16[128,1536]{1,0:T(8,128)(2,1)}) conditional(s32[]{:T(128)} %convert_element_type.768, () %tuple.355, (bf16[128,1536]{1,0:T(8,128)(2,1)S(1)}, f32[2,128]{1,0:T(2,128)}, s32[]{:T(128)}, s32[3,2,3,128]{3,2,1,0:T(4,128)}, bf16[1536,1536]{1,0:T(8,128)(2,1)}) %tuple.356), branch_computations={%region_1.1_spmd, %region_2.4_spmd} | conditional | flops 960245248 | bytes 24682602 | solution.py:129
  191.9 4.4 concatenate.50
  210.1 4.9 collective-permute-start
  218.4 5.2 collective-permute-done
  234.6 28.7 %conditional.12 = (bf16[128,1536]{1,0:T(8,128)(2,1)}) conditional(s32[]{:T(128)} %convert_element_type.768, () %tuple.355, (bf16[128,1536]{1,0:T(8,128)(2,1)S(1)}, f32[2,128]{1,0:T(2,128)}, s32[]{:T(128)}, s32[3,2,3,128]{3,2,1,0:T(4,128)}, bf16[1536,1536]{1,0:T(8,128)(2,1)}) %tuple.356), branch_computations={%region_1.1_spmd, %region_2.4_spmd} | conditional | flops 960245248 | bytes 24682602 | solution.py:129
  245.1 4.4 concatenate.50
  263.3 30.5 %collective-permute-start = (bf16[128,1536]{1,0:T(8,128)(2,1)}, bf16[128,1536]{1,0:T(8,128)(2,1)S(1)}, u32[]{:S(2)}, u32[]{:S(2)}) collective-permute-start(bf16[128,1536]{1,0:T(8,128)(2,1)} %get-tuple-element.1727), channel_id=1, source_target_pairs={{0,8},{8,16},{16,24},{1,9},{9,17},{17,25},{2,10},{10,18},{18,26},{... | collective-permute-start | bytes 1179656 | tf_op jit(solution)/shard_map/while/body/eval_jaxpr/ppermute | solution.py:16
  310.4 26.3 %conditional.13 = (bf16[128,1536]{1,0:T(8,128)(2,1)}) conditional(s32[]{:T(128)} %convert_element_type.769, () %tuple.357, (bf16[128,1536]{1,0:T(8,128)(2,1)S(1)}, f32[2,128]{1,0:T(2,128)}, s32[]{:T(128)}, s32[3,2,3,128]{3,2,1,0:T(4,128)}, bf16[1536,1536]{1,0:T(8,128)(2,1)}) %tuple.358), branch_computations={%region_5.5_spmd, %region_6.0_spmd} | conditional | flops 960245248 | bytes 24223626 | solution.py:134
  318.2 4.4 concatenate.52
  325.2 4.3 concatenate.53
  338.7 33.1 %collective-permute-start = (bf16[128,1536]{1,0:T(8,128)(2,1)}, bf16[128,1536]{1,0:T(8,128)(2,1)S(1)}, u32[]{:S(2)}, u32[]{:S(2)}) collective-permute-start(bf16[128,1536]{1,0:T(8,128)(2,1)} %get-tuple-element.1727), channel_id=1, source_target_pairs={{0,8},{8,16},{16,24},{1,9},{9,17},{17,25},{2,10},{10,18},{18,26},{... | collective-permute-start | bytes 1179656 | tf_op jit(solution)/shard_map/while/body/eval_jaxpr/ppermute | solution.py:16
  387.3 26.3 %conditional.13 = (bf16[128,1536]{1,0:T(8,128)(2,1)}) conditional(s32[]{:T(128)} %convert_element_type.769, () %tuple.357, (bf16[128,1536]{1,0:T(8,128)(2,1)S(1)}, f32[2,128]{1,0:T(2,128)}, s32[]{:T(128)}, s32[3,2,3,128]{3,2,1,0:T(4,128)}, bf16[1536,1536]{1,0:T(8,128)(2,1)}) %tuple.358), branch_computations={%region_5.5_spmd, %region_6.0_spmd} | conditional | flops 960245248 | bytes 24223626 | solution.py:134
  395.1 4.4 concatenate.52
  402.1 4.3 concatenate.53
  415.7 5.8 collective-permute-start
  437.3 4.7 broadcast_in_dim.127.clone
  442.1 4.9 broadcast_in_dim.127
  447.0 497.3 %while.43 = (s32[]{:T(128)}, bf16[128,1536]{0,1:T(8,128)(2,1)}, bf16[128,1536]{0,1:T(8,128)(2,1)}, f32[1536,1536]{1,0:T(8,128)}, f32[1536,1536]{1,0:T(8,128)}, /...) while((s32[]{:T(128)}, bf16[128,1536]{0,1:T(8,128)(2,1)}, ...), condition=%wide.region_31.32_spmd, body=%wide.region_14.31_spmd.sunk | while | flops 4563310592 | bytes 155919184 | solution.py:194
  474.5 50.8 %conditional.15 = (bf16[128,1536]{0,1:T(8,128)(2,1)}, f32[1536,1536]{1,0:T(8,128)}, f32[2,128]{1,0:T(2,128)}) conditional(s32[]{:T(128)} %convert_element_type.771, (f32[1536,1536]{1,0:T(8,128)}, f32[2,128]{1,0:T(2,128)}) %tuple.362, (pred[]{:T(512)}, s32[]{:T(128)}, bf16[2,3,128,1536]{2,3,1,0:T(8,128)(2,1)}, bf16[128,1536]{0,1:T(8,128)(2,1)}, ...), branch_computations={%region_23.23_spmd, %region_24.30_spmd} | conditional | flops 2281655296 | bytes 75604112 | solution.py:179
  489.6 4.4 concatenate.59
  496.6 4.3 concatenate.58
  516.7 8.6 convolution_add_fusion.3
  526.6 5.6 collective-permute-done.3
  537.7 50.8 %conditional.15 = (bf16[128,1536]{0,1:T(8,128)(2,1)}, f32[1536,1536]{1,0:T(8,128)}, f32[2,128]{1,0:T(2,128)}) conditional(s32[]{:T(128)} %convert_element_type.771, (f32[1536,1536]{1,0:T(8,128)}, f32[2,128]{1,0:T(2,128)}) %tuple.362, (pred[]{:T(512)}, s32[]{:T(128)}, bf16[2,3,128,1536]{2,3,1,0:T(8,128)(2,1)}, bf16[128,1536]{0,1:T(8,128)(2,1)}, ...), branch_computations={%region_23.23_spmd, %region_24.30_spmd} | conditional | flops 2281655296 | bytes 75604112 | solution.py:179
  552.8 4.4 concatenate.59
  559.7 4.3 concatenate.58
  579.9 8.6 convolution_add_fusion.3
  588.5 5.0 collective-permute-start.3
  593.6 5.6 collective-permute-done.3
  604.6 50.8 %conditional.15 = (bf16[128,1536]{0,1:T(8,128)(2,1)}, f32[1536,1536]{1,0:T(8,128)}, f32[2,128]{1,0:T(2,128)}) conditional(s32[]{:T(128)} %convert_element_type.771, (f32[1536,1536]{1,0:T(8,128)}, f32[2,128]{1,0:T(2,128)}) %tuple.362, (pred[]{:T(512)}, s32[]{:T(128)}, bf16[2,3,128,1536]{2,3,1,0:T(8,128)(2,1)}, bf16[128,1536]{0,1:T(8,128)(2,1)}, ...), branch_computations={%region_23.23_spmd, %region_24.30_spmd} | conditional | flops 2281655296 | bytes 75604112 | solution.py:179
  619.7 4.4 concatenate.59
  626.7 4.3 concatenate.58
  646.8 8.6 convolution_add_fusion.3
  655.4 90.1 %collective-permute-start.3 = (bf16[128,1536]{0,1:T(8,128)(2,1)}, bf16[128,1536]{0,1:T(8,128)(2,1)S(1)}, u32[]{:S(2)}, u32[]{:S(2)}) collective-permute-start(bf16[128,1536]{0,1:T(8,128)(2,1)} %get-tuple-element.1565), channel_id=1, source_target_pairs={{0,8},{8,16},{16,24},{1,9},{9,17},{17,25},{2,10},{10,18},{18,26},{... | collective-permute-start | bytes 1179656 | tf_op jit(solution)/shard_map/while/body/eval_jaxpr/ppermute | solution.py:16
  745.5 5.6 collective-permute-done.3
  753.8 52.3 %conditional.14 = (bf16[128,1536]{0,1:T(8,128)(2,1)}, f32[1536,1536]{1,0:T(8,128)}, f32[2,128]{1,0:T(2,128)}) conditional(s32[]{:T(128)} %convert_element_type.770, (f32[1536,1536]{1,0:T(8,128)}, f32[2,128]{1,0:T(2,128)}) %tuple.360, (pred[]{:T(512)}, s32[]{:T(128)}, bf16[2,3,128,1536]{2,3,1,0:T(8,128)(2,1)}, bf16[128,1536]{0,1:T(8,128)(2,1)}, ...), branch_computations={%region_15.15_spmd, %region_16.22_spmd} | conditional | flops 2281655296 | bytes 75595864 | solution.py:178
  768.9 4.4 concatenate.57
  775.9 4.3 concatenate.56
  797.3 8.8 convolution_add_fusion.2
  808.9 56.4 %collective-permute-start.3 = (bf16[128,1536]{0,1:T(8,128)(2,1)}, bf16[128,1536]{0,1:T(8,128)(2,1)S(1)}, u32[]{:S(2)}, u32[]{:S(2)}) collective-permute-start(bf16[128,1536]{0,1:T(8,128)(2,1)} %get-tuple-element.1565), channel_id=1, source_target_pairs={{0,8},{8,16},{16,24},{1,9},{9,17},{17,25},{2,10},{10,18},{18,26},{... | collective-permute-start | bytes 1179656 | tf_op jit(solution)/shard_map/while/body/eval_jaxpr/ppermute | solution.py:16
  865.3 5.6 collective-permute-done.3
  873.5 52.3 %conditional.14 = (bf16[128,1536]{0,1:T(8,128)(2,1)}, f32[1536,1536]{1,0:T(8,128)}, f32[2,128]{1,0:T(2,128)}) conditional(s32[]{:T(128)} %convert_element_type.770, (f32[1536,1536]{1,0:T(8,128)}, f32[2,128]{1,0:T(2,128)}) %tuple.360, (pred[]{:T(512)}, s32[]{:T(128)}, bf16[2,3,128,1536]{2,3,1,0:T(8,128)(2,1)}, bf16[128,1536]{0,1:T(8,128)(2,1)}, ...), branch_computations={%region_15.15_spmd, %region_16.22_spmd} | conditional | flops 2281655296 | bytes 75595864 | solution.py:178
  888.7 4.4 concatenate.57
  895.7 4.3 concatenate.56
  917.1 8.8 convolution_add_fusion.2
  928.7 5.8 collective-permute-start.3
  944.3 12.3 %conditional.7 = ((f32[1536,1536]{1,0:T(8,128)}, f32[2,128]{1,0:T(2,128)})) conditional(s32[]{:T(128)} %convert_element_type.515, (f32[1536,1536]{1,0:T(8,128)}, f32[2,128]{1,0:T(2,128)}) %tuple.98, (s32[]{:T(128)}, bf16[3,128,1536]{1,2,0:T(8,128)(2,1)}, f32[2,128]{1,0:T(2,128)}, s32[3,2,3,128]{3,1,2,0:T(2,128)}, pred[]{:T(512)}, ...), branch_computations={%region_40.41_spmd, %region_41.47_spmd} | conditional | flops 2227777280 | bytes 66664800 | solution.py:179
  956.6 6.4 convert_element_type.516
  963.7 51.6 %conditional.6 = ((f32[1536,1536]{1,0:T(8,128)}, f32[2,128]{1,0:T(2,128)})) conditional(s32[]{:T(128)} %convert_element_type.510, (f32[1536,1536]{1,0:T(8,128)}, f32[2,128]{1,0:T(2,128)}) %tuple.96, (s32[]{:T(128)}, bf16[3,128,1536]{1,2,0:T(8,128)(2,1)}, f32[2,128]{1,0:T(2,128)}, s32[3,2,3,128]{3,1,2,0:T(2,128)S(1)}, pred[]{:T(512)}, ...), branch_computations={%region_32.33_spmd, %region_33.39_spmd} | conditional | flops 2227777280 | bytes 66656552 | solution.py:178
  979.4 4.7 concatenate.61
  999.7 9.0 convolution_add_fusion.4
  1015.3 6.5 convert_element_type.513
  1021.8 85.2 %reduce-scatter.5.cloned.1.call-done = bf16[192,1536]{1,0:T(8,128)(2,1)} async-done(((bf16[1536,1536]{1,0:T(8,128)(2,1)}), bf16[192,1536]{1,0:T(8,128)(2,1)}) %reduce-scatter.5.cloned.1.call-update) | async-done | bytes 589840 | tf_op jit(solution)/shard_map/reduce_scatter | solution.py:202
  1108.4 11.6 collective-permute-done.8
  1121.6 16.1 %all-reduce.80 = (f32[2,128]{1,0:T(2,128)S(1)}, bf16[2,128]{1,0:T(2,128)(2,1)S(1)}) all-reduce(f32[2,128]{1,0:T(2,128)} %get-tuple-element.740, f32[2,128]{1,0:T(2,128)S(1)} %copy-done.64), channel_id=1, replica_groups=mesh['pipe'=4,'dp'=8] {'dp'}, use_global_device_ids=true, to_apply=%region_48.49 | all-reduce | flops 512 | bytes 3584 | tf_op jit(solution)/shard_map/psum | solution.py:206
  1145.3 17.5 %reduce-scatter.3.cloned.1.call-done = bf16[192,1536]{1,0:T(8,128)(2,1)} async-done(((bf16[1536,1536]{1,0:T(8,128)(2,1)}), bf16[192,1536]{1,0:T(8,128)(2,1)}) %reduce-scatter.3.cloned.1.call-update) | async-done | bytes 589840 | tf_op jit(solution)/shard_map/reduce_scatter | solution.py:199
  (682 shorter events, 470.7 us)
Async XLA Ops:
  7.2 42.9 %copy-start.19 = (bf16[2,3,128,1536]{3,2,1,0:T(8,128)(2,1)S(1)}, bf16[2,3,128,1536]{3,2,1,0:T(8,128)(2,1)}, u32[]{:S(2)}) copy-start(bf16[2,3,128,1536]{3,2,1,0:T(8,128)(2,1)} %param.33) | copy-start | bytes 7077892
  7.2 56.9 %all-gather.6.cloned.1.call-start = ((), (), s32[]{:S(2)}) async-start(), calls=%async_computation.5 | async-start | bytes 5308416 | tf_op jit(solution)/shard_map/all_gather | solution.py:96
  7.9 108.9 %all-gather.4.cloned.1.call-start = ((), (), s32[]{:S(2)}) async-start(), calls=%async_computation.2 | async-start | bytes 5308416 | tf_op jit(solution)/shard_map/all_gather | solution.py:97
  8.0 16.5 %collective-permute-start.6 = (bf16[192,1536]{1,0:T(8,128)(2,1)}, bf16[192,1536]{1,0:T(8,128)(2,1)S(1)}, u32[]{:S(2)}, u32[]{:S(2)}) collective-permute-start(bf16[192,1536]{1,0:T(8,128)(2,1)} %bitcast.323), channel_id=1, source_target_pairs={{0,8},{8,0},{16,24},{24,16},{1,9},{9,1},{17,25},{25,17},{2,10},{10... | collective-permute-start | bytes 1769480 | tf_op jit(solution)/shard_map/ppermute | solution.py:10
  24.5 14.6 %collective-permute-start.7 = (bf16[192,1536]{1,0:T(8,128)(2,1)S(1)}, bf16[192,1536]{1,0:T(8,128)(2,1)S(1)}, u32[]{:S(2)}, u32[]{:S(2)}) collective-permute-start(bf16[192,1536]{1,0:T(8,128)(2,1)S(1)} %collective-permute-done.6), channel_id=1, source_target_pairs={{0,16},{8,24},{16,0},{24,8},{1,17},{9,25},{17,1},{25,9},{2,18},{10... | collective-permute-start | bytes 1769480 | tf_op jit(solution)/shard_map/ppermute | solution.py:10
  40.0 1067.0 %reduce-scatter.5.cloned.1.call-start = ((), (), s32[]{:S(2)}) async-start(), calls=%async_computation.4 | async-start | bytes 5308416 | tf_op jit(solution)/shard_map/reduce_scatter | solution.py:202
  40.0 5.4 collective-permute-start.4
  45.4 7.2 collective-permute-start.5
  48.2 71.9 %copy-start.65 = (s32[3]{0:T(128)S(1)}, s32[3]{0:T(128)}, u32[]{:S(2)}) copy-start(s32[3]{0:T(128)} %constant.430.clone.1) | copy-start | bytes 40
  129.8 34.7 %collective-permute-start.1 = (bf16[128,1536]{1,0:T(8,128)(2,1)}, bf16[128,1536]{1,0:T(8,128)(2,1)}, u32[]{:S(2)}, u32[]{:S(2)}) collective-permute-start(bf16[128,1536]{1,0:T(8,128)(2,1)} %get-tuple-element.1728), channel_id=1, source_target_pairs={{8,0},{16,8},{24,16},{9,1},{17,9},{25,17},{10,2},{18,10},{26,18},{... | collective-permute-start | bytes 1179656 | tf_op jit(solution)/shard_map/while/body/eval_jaxpr/ppermute | solution.py:16
  138.9 7.0 copy-start.12
  139.0 7.0 copy-start.14
  139.0 7.0 copy-start.16
  139.0 7.0 copy-start.18
  159.8 10.6 collective-permute-start
  180.1 38.3 %collective-permute-start.1 = (bf16[128,1536]{1,0:T(8,128)(2,1)}, bf16[128,1536]{1,0:T(8,128)(2,1)}, u32[]{:S(2)}, u32[]{:S(2)}) collective-permute-start(bf16[128,1536]{1,0:T(8,128)(2,1)} %get-tuple-element.1728), channel_id=1, source_target_pairs={{8,0},{16,8},{24,16},{9,1},{17,9},{25,17},{10,2},{18,10},{26,18},{... | collective-permute-start | bytes 1179656 | tf_op jit(solution)/shard_map/while/body/eval_jaxpr/ppermute | solution.py:16
  189.3 7.0 copy-start.12
  189.3 7.0 copy-start.14
  189.3 7.0 copy-start.16
  189.3 7.0 copy-start.18
  210.1 13.5 %collective-permute-start = (bf16[128,1536]{1,0:T(8,128)(2,1)}, bf16[128,1536]{1,0:T(8,128)(2,1)S(1)}, u32[]{:S(2)}, u32[]{:S(2)}) collective-permute-start(bf16[128,1536]{1,0:T(8,128)(2,1)} %get-tuple-element.1727), channel_id=1, source_target_pairs={{0,8},{8,16},{16,24},{1,9},{9,17},{17,25},{2,10},{10,18},{18,26},{... | collective-permute-start | bytes 1179656 | tf_op jit(solution)/shard_map/while/body/eval_jaxpr/ppermute | solution.py:16
  233.3 63.8 %collective-permute-start.1 = (bf16[128,1536]{1,0:T(8,128)(2,1)}, bf16[128,1536]{1,0:T(8,128)(2,1)}, u32[]{:S(2)}, u32[]{:S(2)}) collective-permute-start(bf16[128,1536]{1,0:T(8,128)(2,1)} %get-tuple-element.1728), channel_id=1, source_target_pairs={{8,0},{16,8},{24,16},{9,1},{17,9},{25,17},{10,2},{18,10},{26,18},{... | collective-permute-start | bytes 1179656 | tf_op jit(solution)/shard_map/while/body/eval_jaxpr/ppermute | solution.py:16
  242.5 7.0 copy-start.12
  242.5 7.0 copy-start.14
  242.5 7.0 copy-start.16
  242.5 7.0 copy-start.18
  263.3 38.1 %collective-permute-start = (bf16[128,1536]{1,0:T(8,128)(2,1)}, bf16[128,1536]{1,0:T(8,128)(2,1)S(1)}, u32[]{:S(2)}, u32[]{:S(2)}) collective-permute-start(bf16[128,1536]{1,0:T(8,128)(2,1)} %get-tuple-element.1727), channel_id=1, source_target_pairs={{0,8},{8,16},{16,24},{1,9},{9,17},{17,25},{2,10},{10,18},{18,26},{... | collective-permute-start | bytes 1179656 | tf_op jit(solution)/shard_map/while/body/eval_jaxpr/ppermute | solution.py:16
  336.7 38.6 %collective-permute-start.1 = (bf16[128,1536]{1,0:T(8,128)(2,1)}, bf16[128,1536]{1,0:T(8,128)(2,1)}, u32[]{:S(2)}, u32[]{:S(2)}) collective-permute-start(bf16[128,1536]{1,0:T(8,128)(2,1)} %get-tuple-element.1728), channel_id=1, source_target_pairs={{8,0},{16,8},{24,16},{9,1},{17,9},{25,17},{10,2},{18,10},{26,18},{... | collective-permute-start | bytes 1179656 | tf_op jit(solution)/shard_map/while/body/eval_jaxpr/ppermute | solution.py:16
  338.7 39.6 %collective-permute-start = (bf16[128,1536]{1,0:T(8,128)(2,1)}, bf16[128,1536]{1,0:T(8,128)(2,1)S(1)}, u32[]{:S(2)}, u32[]{:S(2)}) collective-permute-start(bf16[128,1536]{1,0:T(8,128)(2,1)} %get-tuple-element.1727), channel_id=1, source_target_pairs={{0,8},{8,16},{16,24},{1,9},{9,17},{17,25},{2,10},{10,18},{18,26},{... | collective-permute-start | bytes 1179656 | tf_op jit(solution)/shard_map/while/body/eval_jaxpr/ppermute | solution.py:16
  413.6 11.5 collective-permute-start.1
  415.7 11.4 collective-permute-start
  472.5 54.1 %collective-permute-start.2 = (bf16[128,1536]{0,1:T(8,128)(2,1)}, bf16[128,1536]{0,1:T(8,128)(2,1)}, u32[]{:S(2)}, u32[]{:S(2)}) collective-permute-start(bf16[128,1536]{0,1:T(8,128)(2,1)} %get-tuple-element.1564), channel_id=1, source_target_pairs={{8,0},{16,8},{24,16},{9,1},{17,9},{25,17},{10,2},{18,10},{26,18},{... | collective-permute-start | bytes 1179656 | tf_op jit(solution)/shard_map/while/body/eval_jaxpr/ppermute | solution.py:16
  500.9 6.7 copy-start.7
  515.0 10.3 copy-start.61
  525.3 6.9 collective-permute-start.3
  535.7 57.8 %collective-permute-start.2 = (bf16[128,1536]{0,1:T(8,128)(2,1)}, bf16[128,1536]{0,1:T(8,128)(2,1)}, u32[]{:S(2)}, u32[]{:S(2)}) collective-permute-start(bf16[128,1536]{0,1:T(8,128)(2,1)} %get-tuple-element.1564), channel_id=1, source_target_pairs={{8,0},{16,8},{24,16},{9,1},{17,9},{25,17},{10,2},{18,10},{26,18},{... | collective-permute-start | bytes 1179656 | tf_op jit(solution)/shard_map/while/body/eval_jaxpr/ppermute | solution.py:16
  564.1 6.7 copy-start.7
  578.2 10.3 copy-start.61
  588.5 10.6 collective-permute-start.3
  602.6 142.9 %collective-permute-start.2 = (bf16[128,1536]{0,1:T(8,128)(2,1)}, bf16[128,1536]{0,1:T(8,128)(2,1)}, u32[]{:S(2)}, u32[]{:S(2)}) collective-permute-start(bf16[128,1536]{0,1:T(8,128)(2,1)} %get-tuple-element.1564), channel_id=1, source_target_pairs={{8,0},{16,8},{24,16},{9,1},{17,9},{25,17},{10,2},{18,10},{26,18},{... | collective-permute-start | bytes 1179656 | tf_op jit(solution)/shard_map/while/body/eval_jaxpr/ppermute | solution.py:16
  631.0 6.7 copy-start.5
  631.0 6.7 copy-start.7
  645.1 10.3 copy-start.61
  655.4 95.7 %collective-permute-start.3 = (bf16[128,1536]{0,1:T(8,128)(2,1)}, bf16[128,1536]{0,1:T(8,128)(2,1)S(1)}, u32[]{:S(2)}, u32[]{:S(2)}) collective-permute-start(bf16[128,1536]{0,1:T(8,128)(2,1)} %get-tuple-element.1565), channel_id=1, source_target_pairs={{0,8},{8,16},{16,24},{1,9},{9,17},{17,25},{2,10},{10,18},{18,26},{... | collective-permute-start | bytes 1179656 | tf_op jit(solution)/shard_map/while/body/eval_jaxpr/ppermute | solution.py:16
  780.2 6.7 copy-start.4
  780.2 6.7 copy-start.6
  806.1 59.2 %collective-permute-start.2 = (bf16[128,1536]{0,1:T(8,128)(2,1)}, bf16[128,1536]{0,1:T(8,128)(2,1)}, u32[]{:S(2)}, u32[]{:S(2)}) collective-permute-start(bf16[128,1536]{0,1:T(8,128)(2,1)} %get-tuple-element.1564), channel_id=1, source_target_pairs={{8,0},{16,8},{24,16},{9,1},{17,9},{25,17},{10,2},{18,10},{26,18},{... | collective-permute-start | bytes 1179656 | tf_op jit(solution)/shard_map/while/body/eval_jaxpr/ppermute | solution.py:16
  808.9 62.0 %collective-permute-start.3 = (bf16[128,1536]{0,1:T(8,128)(2,1)}, bf16[128,1536]{0,1:T(8,128)(2,1)S(1)}, u32[]{:S(2)}, u32[]{:S(2)}) collective-permute-start(bf16[128,1536]{0,1:T(8,128)(2,1)} %get-tuple-element.1565), channel_id=1, source_target_pairs={{0,8},{8,16},{16,24},{1,9},{9,17},{17,25},{2,10},{10,18},{18,26},{... | collective-permute-start | bytes 1179656 | tf_op jit(solution)/shard_map/while/body/eval_jaxpr/ppermute | solution.py:16
  900.0 6.7 copy-start.4
  900.0 6.7 copy-start.6
  925.9 11.2 collective-permute-start.2
  928.7 11.4 collective-permute-start.3
  963.0 199.8 %reduce-scatter.3.cloned.1.call-start = ((), (), s32[]{:S(2)}) async-start(), calls=%async_computation.3 | async-start | bytes 5308416 | tf_op jit(solution)/shard_map/reduce_scatter | solution.py:199
  967.6 7.5 copy-start.32
  967.6 7.5 copy-start.34
  967.6 7.5 copy-start.36
  967.6 7.5 copy-start.38
  999.6 9.0 copy-start.45
  999.7 9.0 copy-start.49
  1021.7 99.8 %copy-start.64 = (f32[2,128]{1,0:T(2,128)S(1)}, f32[2,128]{1,0:T(2,128)}, u32[]{:S(2)}) copy-start(f32[2,128]{1,0:T(2,128)} %get-tuple-element.741) | copy-start | bytes 3076
  1107.0 13.1 %collective-permute-start.8 = (bf16[192,1536]{1,0:T(8,128)(2,1)}, bf16[192,1536]{1,0:T(8,128)(2,1)S(1)}, u32[]{:S(2)}, u32[]{:S(2)}) collective-permute-start(bf16[192,1536]{1,0:T(8,128)(2,1)} %reduce-scatter.5.cloned.1.call-done), channel_id=1, source_target_pairs={{0,8},{8,0},{16,24},{24,16},{1,9},{9,1},{17,25},{25,17},{2,10},{10... | collective-permute-start | bytes 1769480 | tf_op jit(solution)/shard_map/ppermute | solution.py:10
  1120.1 42.7 %collective-permute-start.9 = (bf16[192,1536]{1,0:T(8,128)(2,1)S(1)}, bf16[192,1536]{1,0:T(8,128)(2,1)S(1)}, u32[]{:S(2)}, u32[]{:S(2)}) collective-permute-start(bf16[192,1536]{1,0:T(8,128)(2,1)S(1)} %collective-permute-done.8), channel_id=1, source_target_pairs={{0,16},{8,24},{16,0},{24,8},{1,17},{9,25},{17,1},{25,9},{2,18},{10... | collective-permute-start | bytes 1769480 | tf_op jit(solution)/shard_map/ppermute | solution.py:10
  1137.6 3.6 collective-permute-start.10
  1141.2 3.5 collective-permute-start.11
  (68 other events, 212.8 us)
Sparse Core Ops, SparseCore 0:
  9.7 54.3 all-gather.5
  66.3 50.5 all-gather.3
  963.1 143.7 reduce-scatter.4
  1109.1 53.6 reduce-scatter.2
where the time goes:
time: 1190 us; the launch traced here: 1170 us
  starting transfers between devices  259 us (22%)
  waiting for transfers between devices  259 us (22%)
  local copies, waits for them, and re-layouts  203 us (17%)
  other arithmetic  199 us (17%)
  matrix products  166 us (14%)
  loops' own time  55.7 us (5%)
  blocking collectives  16.1 us (1%)
  between operations  14.4 us (1%)
    ppermute x20, starting transfers between devices, shifted(): return lax.ppermute(block, axis, route)  247 us
    concatenate x22, local copies, waits for them, and re-layouts, rotate(): return jnp.concatenate(pieces, axis=-1)  95.3 us
    reduce_scatter x1, waiting for transfers between devices, shards(): lax.psum_scatter(sum_far.astype(jnp.bfloat16), 'dp', scatter_dimension=0,...  85.2 us
    add x33, other arithmetic, rotate(): pieces.append(lower_half * sine_part + upper_half * cosine)  79.7 us
    dot_general x23, matrix products, mixing(): jnp.einsum('qhe,khe->hqk', queries, key_rows, precision=lax.Precision.HIG...  53.6 us
    all_gather x1, waiting for transfers between devices, shards(): lax.all_gather(far_weight, 'dp', axis=0, tiled=True)  52.8 us
    dot_general x6, matrix products, phase_backward(): lax.dot_general(mixed_rows, grad_out, (((0,), (0,)), ((), ())), preferred...  52.4 us
    ppermute x20, waiting for transfers between devices, shifted(): return lax.ppermute(block, axis, route)  48.5 us
  transfers between devices with their start and end apart: 32, of which 21 were waited for; matrix products, arithmetic and copies ran while one was open for 28% of the time, Pallas kernels for 0%

commit v1 on v0

v1 whole, which is shorter than its diff:
```python
import functools
import math

import jax
import jax.numpy as jnp
import numpy as np
from jax import lax
from jax.experimental import pallas as pl
from jax.experimental.pallas import tpu as pltpu
from jax.sharding import PartitionSpec as P

F32 = jnp.float32
BF16 = jnp.bfloat16
VMEM_BYTES = 56 * 1024 * 1024
CORES = 2


def lane_tables(head):
    first = head // 8
    rest = (head - first) // 2
    coord = np.zeros(head, np.int32)
    freq = np.zeros(head, np.float32)
    sign = np.zeros(head, np.float32)
    partner = np.zeros(head, np.int32)
    offset = 0
    for axis, width in enumerate((first, rest, rest)):
        half = width // 2
        for j in range(half):
            low, high = offset + j, offset + j + half
            coord[low] = coord[high] = axis
            freq[low] = freq[high] = 256.0 ** (-2.0 * j / width)
            sign[low], sign[high] = -1.0, 1.0
            partner[low], partner[high] = high, low
        offset += width
    return coord, freq, sign, partner


def swap_lanes(x, partner):
    return jnp.take_along_axis(x, partner, axis=1, mode="promise_in_bounds")


def nt(a, b):
    return lax.dot_general(a, b, (((1,), (1,)), ((), ())), preferred_element_type=F32)


def tn(a, b):
    return lax.dot_general(a, b, (((0,), (0,)), ((), ())), preferred_element_type=F32)


def split(x):
    high = x.astype(BF16)
    return high, (x - high.astype(F32)).astype(BF16)


def fill_tables(tables, cos_ref, sin_ref, gain, first=0):
    for t in range(tables.shape[0]):
        cosine, sine = cos_ref[first + t], sin_ref[first + t]
        tables[t, 0] = cosine * gain[0:1]
        tables[t, 1] = sine * gain[1:2]
        tables[t, 2] = cosine * gain[2:3]
        tables[t, 3] = sine * gain[3:4]


def project(hidden, mixed, weight, out, width):
    def part(i, carry):
        cols = pl.ds(pl.multiple_of(i * width, width), width)
        update = jnp.dot(mixed[...], weight[:, cols], preferred_element_type=F32)
        out[:, cols] = (hidden[:, cols].astype(F32) + update).astype(BF16)
        return carry

    lax.fori_loop(0, out.shape[1] // width, part, 0)


def pull_mixed(grad, weight, grad_mixed, width):
    def part(i, carry):
        cols = pl.ds(pl.multiple_of(i * width, width), width)
        grad_mixed[:, cols] = nt(grad[...], weight[cols, :]).astype(BF16)
        return carry

    lax.fori_loop(0, grad_mixed.shape[1] // width, part, 0)


def head_stage(pairs, hidden, tables, partner):
    values = [hidden[r, c] for _, r, c in pairs]
    wide = [v.astype(F32) for v in values]
    scale = [lax.rsqrt(jnp.mean(x * x, axis=-1, keepdims=True) + 1e-06) for x in wide]
    normed = [x * s for x, s in zip(wide, scale)]
    turned = [swap_lanes(n, partner) for n in normed]
    queries = [split(n * tables[t, 0] + w * tables[t, 1]) for (t, _, _), n, w in zip(pairs, normed, turned)]
    keys = [split(n * tables[t, 2] + w * tables[t, 3]) for (t, _, _), n, w in zip(pairs, normed, turned)]
    scores = [
        nt(jnp.concatenate([qh, ql, qh], axis=1), jnp.concatenate([kh, kh, kl], axis=1))
        for (qh, ql), (kh, kl) in zip(queries, keys)
    ]
    raised = [jnp.exp(s) for s in scores]
    weights = [e * (1.0 / jnp.sum(e, axis=-1, keepdims=True)) for e in raised]
    return values, normed, scale, [q[0] for q in queries], [k[0] for k in keys], weights


def head_pairs(step, groups, tok, head, together):
    cols = [pl.ds(pl.multiple_of((step * together + u) * head, head), head) for u in range(together)]
    return [(t, slice(t * tok, (t + 1) * tok), c) for c in cols for t in range(groups)]


def mix_rows(hidden, tables, partner_ref, mixed, tok, head, together):
    groups = hidden.shape[0] // tok
    partner = partner_ref[...]

    def some(i, carry):
        pairs = head_pairs(i, groups, tok, head, together)
        values, _, _, _, _, weights = head_stage(pairs, hidden, tables, partner)
        rounded = [w.astype(BF16) for w in weights]
        results = [jnp.dot(w, v, preferred_element_type=F32).astype(BF16) for w, v in zip(rounded, values)]
        for (_, r, c), m in zip(pairs, results):
            mixed[r, c] = m
        return carry

    lax.fori_loop(0, hidden.shape[1] // head // together, some, 0)


def pull_rows(
    hidden, grad, grad_mixed, tables, cos_ref, sin_ref, first, gain, partner_ref, counts, sums, out, gain_out, tok, head, together
):
    groups = hidden.shape[0] // tok
    partner = partner_ref[...]
    sums[...] = jnp.zeros(sums.shape, F32)

    def some(i, carry):
        pairs = head_pairs(i, groups, tok, head, together)
        values, normed, scale, queries, keys, weights = head_stage(pairs, hidden, tables, partner)
        above = [grad_mixed[r, c] for _, r, c in pairs]
        grad_weights = [nt(a, v).astype(BF16).astype(F32) for a, v in zip(above, values)]
        if out is not None:
            grad_values = [tn(w.astype(BF16), a) for w, a in zip(weights, above)]
        means = [jnp.sum(g * w, axis=-1, keepdims=True) for g, w in zip(grad_weights, weights)]
        grad_scores = [(w * (g - m)).astype(BF16) for w, g, m in zip(weights, grad_weights, means)]
        grad_q = [jnp.dot(s, k, preferred_element_type=F32) for s, k in zip(grad_scores, keys)]
        grad_k = [tn(s, q) for s, q in zip(grad_scores, queries)]
        swap_q = [swap_lanes(g, partner) for g in grad_q]
        swap_k = [swap_lanes(g, partner) for g in grad_k]
        back_q = [g * cos_ref[first + p[0]] - w * sin_ref[first + p[0]] for p, g, w in zip(pairs, grad_q, swap_q)]
        back_k = [g * cos_ref[first + p[0]] - w * sin_ref[first + p[0]] for p, g, w in zip(pairs, grad_k, swap_k)]
        for t in range(groups):
            mine = [j for j, p in enumerate(pairs) if p[0] == t]
            sums[t, 0] += sum(normed[j] * back_q[j] for j in mine)
            sums[t, 1] += sum(normed[j] * back_k[j] for j in mine)
        if out is not None:
            grad_normed = [q * gain[0:1] + k * gain[2:3] for q, k in zip(back_q, back_k)]
            along = [jnp.mean(n * g, axis=-1, keepdims=True) for n, g in zip(normed, grad_normed)]
            grad_hidden = [
                (v + s * (g - n * a)).astype(BF16).astype(F32)
                for v, s, g, n, a in zip(grad_values, scale, grad_normed, normed, along)
            ]
            for (_, r, c), g in zip(pairs, grad_hidden):
                out[r, c] = (grad[r, c].astype(F32) + g).astype(BF16)
        return carry

    lax.fori_loop(0, hidden.shape[1] // head // together, some, 0)
    factor = 1.0 / math.sqrt(head)
    total_q = sum(counts[t].astype(F32) * jnp.sum(sums[t, 0], axis=0, keepdims=True) for t in range(groups))
    total_k = sum(counts[t].astype(F32) * jnp.sum(sums[t, 1], axis=0, keepdims=True) for t in range(groups))
    gain_out[...] = jnp.concatenate(
        [total_q * factor, total_k, jnp.zeros((gain_out.shape[0] - 2, head), F32)], axis=0
    )


def params(flops, size):
    return dict(
        compiler_params=pltpu.CompilerParams(vmem_limit_bytes=VMEM_BYTES),
        cost_estimate=pl.CostEstimate(flops=flops, bytes_accessed=size, transcendentals=0),
    )


IN_VMEM = pl.BlockSpec(memory_space=pltpu.VMEM)
IN_SMEM = pl.BlockSpec(memory_space=pltpu.SMEM)
ANYWHERE = pl.BlockSpec(memory_space=pl.ANY)


class Plan:
    def __init__(self, clips, out_proj, qk_gains):
        self.depth = lax.axis_size("pipe")
        self.ways = lax.axis_size("dp")
        self.tok = clips.shape[2]
        self.channels = clips.shape[3]
        self.head = qk_gains.shape[-1]
        self.heads = self.channels // self.head
        self.tiles = clips.shape[0] * clips.shape[1]
        self.rows = out_proj.shape[1]
        self.share = self.tiles * self.tok // self.depth
        self.held = max(-(-(p * self.share % self.tok + self.share) // self.tok) for p in range(self.depth))
        self.span = self.held * self.tok
        self.width = math.gcd(self.channels, 512)
        self.chips = self.ways // CORES


def mix_kernel(hidden, cos_ref, sin_ref, gains, partner_ref, mixed, tables, *, plan):
    fill_tables(tables, cos_ref, sin_ref, gains.at[0])
    mix_rows(hidden, tables, partner_ref, mixed, plan.tok, plan.head, plan.heads)


def first_mix(plan, rows, cos, sin, gains, partner):
    pair = CORES
    block = pl.BlockSpec((pair * plan.tok, plan.channels), lambda i: (i, 0))
    angle = pl.BlockSpec((pair, plan.tok, plan.head), lambda i: (i, 0, 0))
    whole = lambda x: pl.BlockSpec(x.shape, lambda i: (0,) * x.ndim)
    return pl.pallas_call(
        functools.partial(mix_kernel, plan=plan),
        grid=(plan.tiles // pair,),
        out_shape=jax.ShapeDtypeStruct(rows.shape, BF16),
        in_specs=[block, angle, angle, whole(gains), whole(partner)],
        out_specs=block,
        scratch_shapes=[pltpu.VMEM((pair, 4, plan.tok, plan.head), F32)],
        name="first_mix",
        **params(4 * rows.size * plan.tok * 4, 4 * rows.size),
    )(rows, cos, sin, gains, partner)


def weight_copies(plan, scalars, blocks, phase, buffer, sems):
    start = pl.multiple_of(scalars[plan.ways + phase], math.gcd(plan.rows, 16))
    return [
        pltpu.make_async_copy(
            block.at[pl.ds(start, plan.rows)],
            buffer.at[pl.ds(pl.multiple_of(scalars[i], math.gcd(plan.rows, 16)), plan.rows)],
            sems.at[i],
        )
        for i, block in enumerate(blocks)
    ]


def chain_kernel(scalars, *refs, plan):
    blocks, refs = refs[: plan.ways], refs[plan.ways :]
    rows, mixed_first, cotangent, cos_ref, sin_ref, gains, partner_ref = refs[:7]
    states, sent, grad_out, grad_sent, gain_out = refs[7:12]
    buffer, start, mixed, grad_in, grad_mixed, tables, sums, sems, row_sems = refs[12:]
    last = plan.depth - 1
    base = scalars[plan.ways + plan.depth]
    window = pl.multiple_of(scalars[plan.ways + plan.depth + 1], math.gcd(plan.share, plan.tok))
    counts = [scalars[plan.ways + plan.depth + 2 + t] for t in range(plan.held)]
    own = pl.ds(pl.multiple_of(base * plan.tok, plan.tok), plan.span)
    loads = [
        pltpu.make_async_copy(source.at[own], target, row_sems.at[i])
        for i, (source, target) in enumerate(((rows, start), (mixed_first, mixed), (cotangent, grad_in)))
    ]
    for load in loads:
        load.start()

    def fetch(phase):
        copies = weight_copies(plan, scalars, blocks, phase, buffer.at[phase % 2], sems.at[phase % 2])
        for copy in copies:
            copy.start()
        return copies

    coming = {phase: fetch(phase) for phase in range(min(2, plan.depth))}
    for load in loads:
        load.wait()
    hidden = start
    for phase in range(plan.depth):
        if phase:
            fill_tables(tables, cos_ref, sin_ref, gains.at[phase], base)
            mix_rows(hidden, tables, partner_ref, mixed, plan.tok, plan.head, plan.heads)
            sent[phase - 1] = mixed[pl.ds(window, plan.share), :]
        for copy in coming[phase]:
            copy.wait()
        if phase < last:
            project(hidden, mixed, buffer.at[phase % 2], states.at[phase], plan.width)
            hidden = states.at[phase]
            if phase + 2 <= last:
                coming[phase + 2] = fetch(phase + 2)
    pull_mixed(grad_in, buffer.at[last % 2], grad_mixed, plan.width)
    pull_rows(
        hidden, grad_in, grad_mixed, tables, cos_ref, sin_ref, base, gains.at[last], partner_ref, counts, sums,
        grad_out, gain_out, plan.tok, plan.head, plan.heads,
    )
    grad_sent[...] = grad_out[pl.ds(window, plan.share), :]


def chain(plan, scalars, blocks, rows, mixed_first, cotangent, cos, sin, gains, partner):
    shape = jax.ShapeDtypeStruct
    return pl.pallas_call(
        functools.partial(chain_kernel, plan=plan),
        out_shape=(
            shape((plan.depth - 1, plan.span, plan.channels), BF16),
            shape((plan.depth - 1, plan.share, plan.channels), BF16),
            shape((plan.span, plan.channels), BF16),
            shape((plan.share, plan.channels), BF16),
            shape((8, plan.head), F32),
        ),
        in_specs=[IN_SMEM] + [ANYWHERE] * (plan.ways + 3) + [IN_VMEM] * 4,
        out_specs=(IN_VMEM,) * 5,
        scratch_shapes=[
            pltpu.VMEM((2, plan.channels, plan.channels), BF16),
            pltpu.VMEM((plan.span, plan.channels), BF16),
            pltpu.VMEM((plan.span, plan.channels), BF16),
            pltpu.VMEM((plan.span, plan.channels), BF16),
            pltpu.VMEM((plan.span, plan.channels), BF16),
            pltpu.VMEM((plan.held, 4, plan.tok, plan.head), F32),
            pltpu.VMEM((plan.held, 2, plan.tok, plan.head), F32),
            pltpu.SemaphoreType.DMA((2, plan.ways)),
            pltpu.SemaphoreType.DMA((3,)),
        ],
        name="chain",
        **params(2 * plan.depth * plan.span * plan.channels * plan.channels * 2, 2 * plan.depth * plan.channels**2),
    )(scalars, *blocks, rows, mixed_first, cotangent, cos, sin, gains, partner)


def back_kernel(scalars, *refs, plan, phase):
    blocks, refs = refs[: plan.ways], refs[plan.ways :]
    hidden_any, grad_in, cos_ref, sin_ref, gains, partner_ref = refs[:6]
    if phase:
        grad_out, grad_sent, gain_out = refs[6:9]
        refs = refs[9:]
    else:
        grad_out, gain_out = None, refs[6]
        refs = refs[7:]
    buffer, hidden, grad_mixed, tables, sums, sems, row_sem = refs
    base = scalars[plan.ways + plan.depth]
    window = pl.multiple_of(scalars[plan.ways + plan.depth + 1], math.gcd(plan.share, plan.tok))
    counts = [scalars[plan.ways + plan.depth + 2 + t] for t in range(plan.held)]
    copies = weight_copies(plan, scalars, blocks, phase, buffer, sems)
    for copy in copies:
        copy.start()
    if phase:
        source = hidden_any.at[phase - 1]
    else:
        source = hidden_any.at[pl.ds(pl.multiple_of(base * plan.tok, plan.tok), plan.span)]
    load = pltpu.make_async_copy(source, hidden, row_sem.at[0])
    load.start()
    fill_tables(tables, cos_ref, sin_ref, gains.at[phase], base)
    for copy in copies:
        copy.wait()
    pull_mixed(grad_in, buffer, grad_mixed, plan.width)
    load.wait()
    pull_rows(
        hidden, grad_in, grad_mixed, tables, cos_ref, sin_ref, base, gains.at[phase], partner_ref, counts, sums,
        grad_out, gain_out, plan.tok, plan.head, plan.heads,
    )
    if phase:
        grad_sent[...] = grad_out[pl.ds(window, plan.share), :]


def back(plan, phase, scalars, blocks, hidden, grad_in, cos, sin, gains, partner):
    shape = jax.ShapeDtypeStruct
    grads = (shape((plan.span, plan.channels), BF16), shape((plan.share, plan.channels), BF16)) if phase else ()
    return pl.pallas_call(
        functools.partial(back_kernel, plan=plan, phase=phase),
        out_shape=grads + (shape((8, plan.head), F32),),
        in_specs=[IN_SMEM] + [ANYWHERE] * (plan.ways + 1) + [IN_VMEM] * 5,
        out_specs=(IN_VMEM,) * (len(grads) + 1),
        scratch_shapes=[
            pltpu.VMEM((plan.channels, plan.channels), BF16),
            pltpu.VMEM((plan.span, plan.channels), BF16),
            pltpu.VMEM((plan.span, plan.channels), BF16),
            pltpu.VMEM((plan.held, 4, plan.tok, plan.head), F32),
            pltpu.VMEM((plan.held, 2, plan.tok, plan.head), F32),
            pltpu.SemaphoreType.DMA((plan.ways,)),
            pltpu.SemaphoreType.DMA((1,)),
        ],
        name="back",
        **params(6 * plan.span * plan.channels * plan.channels, 3 * plan.channels**2),
    )(scalars, *blocks, hidden, grad_in, cos, sin, gains, partner)


def turn_kernel(place, *refs, plan):
    own, mixed_first, received = refs[0], refs[1], refs[2 : plan.depth + 1]
    out, gathered, sems = refs[plan.depth + 1 :]
    me = place[0]

    def gather(first):
        copies = []
        for k in range(plan.depth):
            if first:
                source = mixed_first.at[pl.ds(k * plan.share, plan.share)]
            elif k:
                source = received[k - 1]
            else:
                source = own.at[jnp.maximum(me, 1) - 1]
            copies.append(pltpu.make_async_copy(source, gathered.at[pl.ds(k * plan.share, plan.share)], sems.at[k]))
        for copy in copies:
            copy.start()
        for copy in copies:
            copy.wait()

    pl.when(me == 0)(lambda: gather(True))
    pl.when(me != 0)(lambda: gather(False))

    def part(i, carry):
        cols = pl.ds(pl.multiple_of(i * plan.width, plan.width), plan.width)
        out[cols, :] = gathered[:, cols].T
        return carry

    lax.fori_loop(0, plan.channels // plan.width, part, 0)


def turn(plan, place, own, mixed_first, received):
    total = plan.depth * plan.share
    return pl.pallas_call(
        functools.partial(turn_kernel, plan=plan),
        out_shape=jax.ShapeDtypeStruct((plan.channels, total), BF16),
        in_specs=[IN_SMEM] + [ANYWHERE] * (plan.depth + 1),
        out_specs=IN_VMEM,
        scratch_shapes=[pltpu.VMEM((total, plan.channels), BF16), pltpu.SemaphoreType.DMA((plan.depth,))],
        name="turn",
        **params(0, 4 * total * plan.channels),
    )(place, own, mixed_first, *received)


def term_kernel(place, *refs, plan, theirs):
    turned, cotangent, refs = refs[0], refs[1], refs[2:]
    sources = [refs[i * plan.depth : (i + 1) * plan.depth] for i in range(plan.depth - 1)]
    refs = refs[plan.depth * (plan.depth - 1) :]
    if theirs:
        out, grads, sems = refs
    else:
        partial, out, grads, sems = refs
    me, core = place[0], place[1]

    def gather(phase):
        copies = []
        for k in range(plan.depth):
            if phase == plan.depth - 1:
                source = cotangent.at[pl.ds((phase ^ k) * plan.share, plan.share)]
            else:
                source = sources[phase][k]
            copies.append(pltpu.make_async_copy(source, grads.at[pl.ds(k * plan.share, plan.share)], sems.at[k]))
        for copy in copies:
            copy.start()
        for copy in copies:
            copy.wait()

    for phase in range(plan.depth):
        pl.when(me == phase)(functools.partial(gather, phase))
    which = 1 - core if theirs else core

    def part(chip, carry):
        here = pl.multiple_of((chip * CORES + which) * plan.rows, math.gcd(plan.rows, 16))
        term = jnp.dot(turned[pl.ds(here, plan.rows), :], grads[...], preferred_element_type=F32)
        if not theirs:
            term = term + partial[chip].astype(F32)
        out[chip] = term.astype(BF16)
        return carry

    lax.fori_loop(0, plan.chips, part, 0)


def term(plan, place, turned, cotangent, sources, partial=None):
    total = plan.depth * plan.share
    flat = [x for phase in sources for x in phase]
    extra = [] if partial is None else [partial]
    return pl.pallas_call(
        functools.partial(term_kernel, plan=plan, theirs=partial is None),
        out_shape=jax.ShapeDtypeStruct((plan.chips, plan.rows, plan.channels), BF16),
        in_specs=[IN_SMEM, IN_VMEM] + [ANYWHERE] * (1 + len(flat)) + [IN_VMEM] * len(extra),
        out_specs=IN_VMEM,
        scratch_shapes=[pltpu.VMEM((total, plan.channels), BF16), pltpu.SemaphoreType.DMA((plan.depth,))],
        name="term",
        **params(total * plan.channels**2, 4 * plan.channels**2),
    )(place, turned, cotangent, *flat, *extra)


def along_pipe(x, k):
    return lax.ppermute(x, "pipe", [(i, i ^ k) for i in range(lax.axis_size("pipe"))])


def to_place(x, k, place):
    return lax.ppermute(x, "pipe", [(place ^ k, place)])


def along_chips(x, k):
    return lax.ppermute(x, "dp", [(i, i ^ (CORES * k)) for i in range(lax.axis_size("dp"))])


def other_core(x):
    return lax.ppermute(x, "dp", [(i, i ^ 1) for i in range(lax.axis_size("dp"))])


def spread_near(block, depth):
    return {1 << bit: along_pipe(block, 1 << bit) for bit in range(depth.bit_length() - 1)}


def spread_far(block, near, depth):
    bits = depth.bit_length() - 1
    part = block.shape[0] // max(bits, 1)
    got = {0: block, **near}
    for k in sorted(range(1, depth), key=lambda k: k.bit_count()):
        if k in got:
            continue
        pieces = []
        for i in range(bits):
            order = [(i + b) % bits for b in range(bits)]
            bit = [b for b in order if k >> b & 1][-1]
            pieces.append(along_pipe(got[k ^ (1 << bit)][i * part : (i + 1) * part], 1 << bit))
        got[k] = jnp.concatenate(pieces, axis=0)
    return [got[k] for k in range(depth)]


def gather_weights(plan, own, chip):
    chips = plan.chips
    order = [sorted((b for b in range(chips) if b != c), key=lambda b: (abs(b - c), b ^ c)) for c in range(chips)]
    up = down = block = own
    arrived = {}
    stacks, whose = [], []
    for step in range(1, chips + 1):
        near = spread_near(block, plan.depth)
        if step < chips:
            up = lax.ppermute(up, "dp", [(i, i + CORES) for i in range(plan.ways - CORES)])
            down = lax.ppermute(down, "dp", [(i + CORES, i) for i in range(plan.ways - CORES)])
            keys = list(near)
            up, down, *held = lax.optimization_barrier((up, down, *near.values()))
            near = dict(zip(keys, held))
            arrived[step, -1], arrived[step, 1] = up, down
        stacks.append(jnp.concatenate(spread_far(block, near, plan.depth), axis=0))
        source = [c if step == 1 else order[c][step - 2] for c in range(chips)]
        whose.append(jnp.asarray(source, jnp.int32)[chip])
        if step < chips:
            places = {}
            for c in range(chips):
                b = order[c][step - 1]
                places.setdefault((abs(b - c), 1 if b > c else -1), []).append(c)
            (first, _), *others = places.items()
            block = arrived[first]
            for key, members in others:
                here = functools.reduce(jnp.logical_or, [chip == c for c in members])
                block = jnp.where(here, arrived[key], block)
    return stacks, whose


def shards(clips, positions, out_proj, qk_gains, cotangent):
    plan = Plan(clips, out_proj, qk_gains)
    depth, last = plan.depth, plan.depth - 1
    place = lax.axis_index("pipe")
    member = lax.axis_index("dp")
    chip, core = member // CORES, member % CORES

    stacks, whose = gather_weights(plan, out_proj[0], chip)
    blocks = stacks + [other_core(stack) for stack in stacks]
    starts = [(w * CORES + core) * plan.rows for w in whose] + [(w * CORES + 1 - core) * plan.rows for w in whose]

    first_row = place * plan.share
    base = jnp.minimum(first_row // plan.tok, plan.tiles - plan.held)
    tile_starts = [(base + t) * plan.tok for t in range(plan.held)]
    counts = [((s >= first_row) & (s < first_row + plan.share)).astype(jnp.int32) for s in tile_starts]
    scalars = jnp.stack(
        starts + [(place ^ s) * plan.rows for s in range(depth)] + [base, first_row - base * plan.tok] + counts
    ).astype(jnp.int32)

    coord, freq, sign, partner = lane_tables(plan.head)
    spots = positions.reshape(3, plan.tiles, plan.tok, 1).astype(F32)
    angles = jnp.where(coord == 0, spots[0], jnp.where(coord == 1, spots[1], spots[2])) * freq
    cos, sin = jnp.cos(angles), jnp.sin(angles) * sign
    gain_table = lax.all_gather(qk_gains[0], "pipe").astype(F32)
    factor = 1.0 / math.sqrt(plan.head)
    swapped = gain_table[..., partner]
    queries, keys = gain_table[:, 0] * factor, gain_table[:, 1]
    rows_of = [queries, swapped[:, 0] * factor, keys, swapped[:, 1]]
    gains = jnp.stack(rows_of + [jnp.zeros_like(keys)] * 4, axis=1)
    partners = jnp.broadcast_to(jnp.asarray(partner), (plan.tok, plan.head))
    setting = (cos, sin, gains, partners)

    rows = clips.reshape(plan.tiles * plan.tok, plan.channels)
    last_grad = cotangent.reshape(plan.tiles * plan.tok, plan.channels)
    mixed_first = first_mix(plan, rows, *setting)
    states, mixed, grad, grad_window, gain = chain(plan, scalars, blocks, rows, mixed_first, last_grad, *setting)
    gain_terms = {last: gain}
    sources = {}
    received = []
    for k in range(1, depth):
        chosen = lax.dynamic_index_in_dim(mixed, jnp.maximum(place ^ k, 1) - 1, 0, keepdims=False)
        pairs = [(i, i ^ k) for i in range(depth) if i ^ k]
        received.append(lax.ppermute(chosen, "pipe", pairs))
    for phase in range(last - 1, -1, -1):
        sources[phase] = [grad_window] + [to_place(grad_window, k, phase) for k in range(1, depth)]
        if phase:
            grad, grad_window, gain = back(plan, phase, scalars, blocks, states, grad, *setting)
        else:
            (gain,) = back(plan, phase, scalars, blocks, rows, grad, *setting)
        gain_terms[phase] = gain

    where = jnp.stack([place, core]).astype(jnp.int32)
    turned = turn(plan, where, mixed, mixed_first, received)
    flat = [sources[phase] for phase in range(last)]
    theirs = term(plan, where, turned, last_grad, flat)
    mine = term(plan, where, turned, last_grad, flat, other_core(theirs))
    total = lax.dynamic_index_in_dim(mine, chip, 0, keepdims=False).astype(F32)
    for k in range(1, plan.chips):
        piece = lax.dynamic_index_in_dim(mine, chip ^ k, 0, keepdims=False)
        total = total + along_chips(piece, k).astype(F32)

    gain_sums = lax.psum(jnp.stack([gain_terms[s][:2] for s in range(depth)]), ("pipe", "dp"))
    own_gains = lax.dynamic_index_in_dim(gain_sums, place, 0, keepdims=False)
    return (total[None], own_gains[None])


def solution(mesh):
    placed = (
        P(None, None, "dp", None),
        P(None, None, None, "dp"),
        P("pipe", "dp", None),
        P("pipe", None, None),
        P(None, None, "dp", None),
    )
    return jax.shard_map(
        shards,
        mesh=mesh,
        in_specs=placed,
        out_specs=(P("pipe", "dp", None), P("pipe", None, None)),
        check_vma=False,
    )
```

time: 1190 us -> 382 us (0.32); the launches traced: 1170 us -> 377 us
  starting transfers between devices: 259 us -> 61.7 us
  other arithmetic: 199 us -> 8.4 us
  local copies, waits for them, and re-layouts: 203 us -> 24.8 us
  matrix products: 166 us -> 0 us
  waiting for transfers between devices: 259 us -> 104 us
  Pallas kernels: 0 us -> 94.2 us
  blocking collectives: 16.1 us -> 80.3 us
  loops' own time: 55.7 us -> 0 us
    ppermute x28 -> x42, starting transfers between devices: 259 us -> 61.7 us  [the longest x16 18.7 us: along_pipe(): lax.ppermute(x, 'pipe', [(i, i ^ k) for i in range(lax.axis_size('pipe'))])]
    dot_general x62 -> x0, matrix products: 166 us -> none  [the longest x23 53.6 us: mixing(): jnp.einsum('qhe,khe->hqk', queries, key_rows, precision=lax.Precision.HIG...]
    reduce_scatter x2 -> x0, waiting for transfers between devices: 103 us -> none  [the longest x1 85.2 us: shards(): lax.psum_scatter(sum_far.astype(jnp.bfloat16), 'dp', scatter_dimension=0,...]
    pallas_call x0 -> x8, Pallas kernels: none -> 94.2 us  [the longest x3 37 us: back(): pl.pallas_call(functools.partial(back_kernel, plan=plan, phase=phase), ou...]
    concatenate x22 -> x4, local copies, waits for them, and re-layouts: 95.3 us -> 2.26 us  [gather_weights(): stacks.append(jnp.concatenate(spread_far(block, near, plan.depth), axis=0))]
    add x39 -> x0, other arithmetic: 83.6 us -> none  [the longest x33 79.7 us: rotate(): pieces.append(lower_half * sine_part + upper_half * cosine)]
    all_gather x2 -> x0, waiting for transfers between devices: 63.7 us -> none  [the longest x1 52.8 us: shards(): lax.all_gather(far_weight, 'dp', axis=0, tiled=True)]
    psum x1, blocking collectives: 16.1 us -> 71.8 us  [shards(): lax.psum(jnp.stack([gain_terms[s][:2] for s in range(depth)]), ('pipe', '...]
  transfers between devices with their start and end apart: 32 -> 42, of which waited for: 21 -> 12; matrix products, arithmetic and copies ran while one was open for 28% -> 7% of each run, Pallas kernels for 0% -> 7%
where the time goes in v1:
time: 382 us; the launch traced here: 377 us
  waiting for transfers between devices  104 us (27%)
  Pallas kernels  94.2 us (25%)
  blocking collectives  80.3 us (21%)
  starting transfers between devices  61.7 us (16%)
  local copies, waits for them, and re-layouts  24.8 us (6%)
  other arithmetic  8.4 us (2%)
    psum x1, blocking collectives, shards(): lax.psum(jnp.stack([gain_terms[s][:2] for s in range(depth)]), ('pipe', '...  71.8 us
    ppermute x16, waiting for transfers between devices, along_pipe(): lax.ppermute(x, 'pipe', [(i, i ^ k) for i in range(lax.axis_size('pipe'))])  56.5 us
    pallas_call x3, Pallas kernels, back(): pl.pallas_call(functools.partial(back_kernel, plan=plan, phase=phase), ou...  37 us
    pallas_call x1, Pallas kernels, chain(): pl.pallas_call(functools.partial(chain_kernel, plan=plan), out_shape=(sha...  27.9 us
    ppermute x9, waiting for transfers between devices, to_place(): return lax.ppermute(x, 'pipe', [(place ^ k, place)])  23.2 us
    ppermute x3, waiting for transfers between devices, shards(): received.append(lax.ppermute(chosen, 'pipe', pairs))  19.8 us
    ppermute x16, starting transfers between devices, along_pipe(): lax.ppermute(x, 'pipe', [(i, i ^ k) for i in range(lax.axis_size('pipe'))])  18.7 us
    pallas_call x2, Pallas kernels, term(): pl.pallas_call(functools.partial(term_kernel, plan=plan, theirs=partial i...  15.2 us
  transfers between devices with their start and end apart: 42, of which 12 were waited for; matrix products, arithmetic and copies ran while one was open for 7% of the time, Pallas kernels for 7%

profile of v1, /device:TPU:0, one launch (start us, length us, event | category | flops | bytes accessed | tf_op | source)
XLA Modules:
  0.0 377.0 jit_solution(8602184224383891251)
XLA Ops:
  0.6 3.0 collective-permute-start.3
  3.7 1.5 collective-permute-start.2
  5.2 1.3 collective-permute-start.1
  6.4 4.6 %collective-permute-start = (bf16[192,1536]{1,0:T(8,128)(2,1)}, bf16[192,1536]{1,0:T(8,128)(2,1)S(1)}, u32[]{:S(2)}, u32[]{:S(2)}) collective-permute-start(bf16[192,1536]{1,0:T(8,128)(2,1)} %bitcast.60), channel_id=1, source_target_pairs={{0,2},{1,3},{2,4},{3,5},{4,6},{5,7},{8,10},{9,11},{10,12},{11,13},... | collective-permute-start | bytes 1769480 | tf_op jit(solution)/shard_map/ppermute | solution.py:505
  11.1 1.9 constant_dynamic-update-slice_fusion.4
  13.0 4.2 %collective-permute-done.3 = bf16[192,1536]{1,0:T(8,128)(2,1)S(1)} collective-permute-done((bf16[192,1536]{1,0:T(8,128)(2,1)}, bf16[192,1536]{1,0:T(8,128)(2,1)S(1)}, u32[]{:S(2)}, u32[]{:S(2)}) %collective-permute-start.3) | collective-permute-done | bytes 589856 | tf_op jit(solution)/shard_map/ppermute | solution.py:461
  17.2 1.5 collective-permute-done.2
  18.7 3.1 collective-permute-done.1
  21.8 1.3 collective-permute-done
  23.6 4.3 %collective-permute-start.6 = (bf16[192,1536]{1,0:T(8,128)(2,1)S(1)}, bf16[192,1536]{1,0:T(8,128)(2,1)S(1)}, u32[]{:S(2)}, u32[]{:S(2)}) collective-permute-start(bf16[192,1536]{1,0:T(8,128)(2,1)S(1)} %collective-permute-done), channel_id=1, source_target_pairs={{0,2},{1,3},{2,4},{3,5},{4,6},{5,7},{8,10},{9,11},{10,12},{11,13},... | collective-permute-start | bytes 1769480 | tf_op jit(solution)/shard_map/ppermute | solution.py:505
  28.0 1.3 collective-permute-start.7
  29.4 1.6 collective-permute-start.9
  31.6 0.9 constant_dynamic-update-slice_fusion.3
  32.5 1.5 collective-permute-start.5
  34.0 0.9 constant_dynamic-update-slice_fusion.2
  35.6 14.2 %collective-permute-done.5 = bf16[96,1536]{1,0:T(8,128)(2,1)S(1)} collective-permute-done((bf16[96,1536]{1,0:T(8,128)(2,1)S(1)}, bf16[96,1536]{1,0:T(8,128)(2,1)S(1)}, u32[]{:S(2)}, u32[]{:S(2)}) %collective-permute-start.5) | collective-permute-done | bytes 294944 | tf_op jit(solution)/shard_map/ppermute | solution.py:461
  51.2 4.3 %collective-permute-start.12 = (bf16[192,1536]{1,0:T(8,128)(2,1)S(1)}, bf16[192,1536]{1,0:T(8,128)(2,1)S(1)}, u32[]{:S(2)}, u32[]{:S(2)}) collective-permute-start(bf16[192,1536]{1,0:T(8,128)(2,1)S(1)} %collective-permute-done.6), channel_id=1, source_target_pairs={{0,2},{1,3},{2,4},{3,5},{4,6},{5,7},{8,10},{9,11},{10,12},{11,13},... | collective-permute-start | bytes 1769480 | tf_op jit(solution)/shard_map/ppermute | solution.py:505
  55.5 1.3 collective-permute-start.13
  56.8 1.1 constant_dynamic-update-slice_fusion.14
  57.9 1.5 collective-permute-start.15
  60.0 1.6 collective-permute-start.11
  61.6 14.5 %collective-permute-done.11 = bf16[96,1536]{1,0:T(8,128)(2,1)S(1)} collective-permute-done((bf16[96,1536]{1,0:T(8,128)(2,1)S(1)}, bf16[96,1536]{1,0:T(8,128)(2,1)S(1)}, u32[]{:S(2)}, u32[]{:S(2)}) %collective-permute-start.11) | collective-permute-done | bytes 294944 | tf_op jit(solution)/shard_map/ppermute | solution.py:461
  76.2 1.4 constant_dynamic-update-slice_fusion.19
  78.2 0.9 collective-permute-start.18
  79.1 1.2 collective-permute-start.16
  80.3 0.9 constant_dynamic-update-slice_fusion.13
  81.2 1.6 collective-permute-start.17
  82.7 0.9 constant_dynamic-update-slice_fusion.12
  83.6 16.1 %collective-permute-done.16 = bf16[96,1536]{1,0:T(8,128)(2,1)S(1)} collective-permute-done((bf16[96,1536]{1,0:T(8,128)(2,1)S(1)}, bf16[96,1536]{1,0:T(8,128)(2,1)S(1)}, u32[]{:S(2)}, u32[]{:S(2)}) %collective-permute-start.16) | collective-permute-done | bytes 294944 | tf_op jit(solution)/shard_map/ppermute | solution.py:461
  99.7 0.8 constant_dynamic-update-slice_fusion.11
  102.5 1.0 collective-permute-start.20
  103.5 0.9 constant_dynamic-update-slice_fusion.18
  104.4 0.9 constant_dynamic-update-slice_fusion.17
  105.2 6.0 %collective-permute-done.20 = bf16[96,1536]{1,0:T(8,128)(2,1)S(1)} collective-permute-done((bf16[96,1536]{1,0:T(8,128)(2,1)S(1)}, bf16[96,1536]{1,0:T(8,128)(2,1)S(1)}, u32[]{:S(2)}, u32[]{:S(2)}) %collective-permute-start.20) | collective-permute-done | bytes 294944 | tf_op jit(solution)/shard_map/ppermute | solution.py:461
  116.5 8.4 %all_gather.3 = bf16[4,2,128]{2,1,0:T(2,128)(2,1)S(1)} all-gather(bf16[1,2,128]{2,1,0:T(2,128)(2,1)S(1)} %copy-done.26), channel_id=1, replica_groups=mesh['pipe'=4,'dp'=8] {'pipe'}, dimensions={0}, use_global_device_ids=true | all-gather | bytes 2560 | tf_op jit(solution)/shard_map/all_gather | solution.py:550
  127.5 2.7 sine_multiply_fusion
  130.8 9.4 %first_mix.1.refs_9_.refs_1_ = bf16[768,1536]{1,0:T(8,128)(2,1)} custom-call(bf16[768,1536]{1,0:T(8,128)(2,1)} %bitcast.54, f32[6,128,128]{2,1,0:T(8,128)} %get-tuple-element.61.cos_ref.refs_11_.refs_10_, f32[6,128,128]{2,1,0:T(8,128)} %get-tuple-element.60.sin_ref.refs_12_.refs_11_, f32[4,8,128]{2,1,0:T(8,128)} %stack.112.gains.refs_13_.refs_12_, ...), custom_call_target="tpu_custom_call" | custom-call | flops 2415919104 | bytes 4718592 | tf_op jit(solution)/shard_map/first_mix/pallas_call | solution.py:206
  140.2 27.9 %chain.1 = (bf16[3,256,1536]{2,1,0:T(8,128)(2,1)}, bf16[3,192,1536]{2,1,0:T(8,128)(2,1)}, bf16[256,1536]{1,0:T(8,128)(2,1)}, bf16[192,1536]{1,0:T(8,128)(2,1)}, f32[8,128]{1,0:T(8,128)}) custom-call(s32[16]{0:T(128)} %stack.110.scalars, bf16[768,1536]{1,0:T(8,128)(2,1)} %constant_dynamic-update-slice_fusion.refs_0_, bf16[768,1536]{1,0:T(8,128)(2,1)} %copy-done, ...), custom_call_target="tpu_custom_call" | custom-call | flops 9663676416 | bytes 18874368 | tf_op jit(solution)/shard_map/chain/pallas_call | solution.py:279
  168.1 12.7 %back.3 = (bf16[256,1536]{1,0:T(8,128)(2,1)}, bf16[192,1536]{1,0:T(8,128)(2,1)}, f32[8,128]{1,0:T(8,128)}) custom-call(s32[16]{0:T(128)} %stack.110.scalars, bf16[768,1536]{1,0:T(8,128)(2,1)} %constant_dynamic-update-slice_fusion.refs_0_, bf16[768,1536]{1,0:T(8,128)(2,1)} %copy-done, bf16[768,1536]{1,0:T(8,128)(2,1)} %constant_dynamic-update-slice_fusion.10.refs_2_, ...), custom_call_target="tpu_custom_call" | custom-call | flops 3623878656 | bytes 7077888 | tf_op jit(solution)/shard_map/back/pallas_call | solution.py:344
  180.8 13.0 %back.4 = (bf16[256,1536]{1,0:T(8,128)(2,1)}, bf16[192,1536]{1,0:T(8,128)(2,1)}, f32[8,128]{1,0:T(8,128)}) custom-call(s32[16]{0:T(128)} %stack.110.scalars, bf16[768,1536]{1,0:T(8,128)(2,1)} %constant_dynamic-update-slice_fusion.refs_0_, bf16[768,1536]{1,0:T(8,128)(2,1)} %copy-done, bf16[768,1536]{1,0:T(8,128)(2,1)} %constant_dynamic-update-slice_fusion.10.refs_2_, ...), custom_call_target="tpu_custom_call" | custom-call | flops 3623878656 | bytes 7077888 | tf_op jit(solution)/shard_map/back/pallas_call | solution.py:344
  193.8 1.4 collective-permute-start.31
  195.2 1.3 collective-permute-start.30
  196.5 1.3 collective-permute-start.29
  198.7 5.1 %collective-permute-start.28 = (bf16[192,1536]{1,0:T(8,128)(2,1)S(1)}, bf16[192,1536]{1,0:T(8,128)(2,1)S(1)}, u32[]{:S(2)}, u32[]{:S(2)}) collective-permute-start(bf16[192,1536]{1,0:T(8,128)(2,1)S(1)} %get-tuple-element.57), channel_id=1, source_target_pairs={{0,24},{8,16},{16,8},{1,25},{9,17},{17,9},{2,26},{10,18},{18,10},{... | collective-permute-start | bytes 1769480 | tf_op jit(solution)/shard_map/ppermute | solution.py:569
  203.8 7.0 %collective-permute-done.31.refs_5_ = bf16[192,1536]{1,0:T(8,128)(2,1)S(1)} collective-permute-done((bf16[192,1536]{1,0:T(8,128)(2,1)}, bf16[192,1536]{1,0:T(8,128)(2,1)S(1)}, u32[]{:S(2)}, u32[]{:S(2)}) %collective-permute-start.31) | collective-permute-done | bytes 589856 | tf_op jit(solution)/shard_map/ppermute | solution.py:465
  210.7 1.3 collective-permute-start.27
  212.1 11.3 %collective-permute-done.30.refs_4_ = bf16[192,1536]{1,0:T(8,128)(2,1)} collective-permute-done((bf16[192,1536]{1,0:T(8,128)(2,1)}, bf16[192,1536]{1,0:T(8,128)(2,1)}, u32[]{:S(2)}, u32[]{:S(2)}) %collective-permute-start.30) | collective-permute-done | bytes 589856 | tf_op jit(solution)/shard_map/ppermute | solution.py:465
  223.4 1.3 collective-permute-start.26
  225.5 1.3 collective-permute-start.32
  227.5 19.8 %collective-permute-done.27.refs_3_ = bf16[192,1536]{1,0:T(8,128)(2,1)S(1)} collective-permute-done((bf16[192,1536]{1,0:T(8,128)(2,1)S(1)}, bf16[192,1536]{1,0:T(8,128)(2,1)S(1)}, u32[]{:S(2)}, u32[]{:S(2)}) %collective-permute-start.27) | collective-permute-done | bytes 589856 | tf_op jit(solution)/shard_map/ppermute | solution.py:569
  247.3 4.4 %collective-permute-start.36 = (bf16[192,1536]{1,0:T(8,128)(2,1)S(1)}, bf16[192,1536]{1,0:T(8,128)(2,1)S(1)}, u32[]{:S(2)}, u32[]{:S(2)}) collective-permute-start(bf16[192,1536]{1,0:T(8,128)(2,1)S(1)} %copy-done.3), channel_id=1, source_target_pairs={{0,16},{1,17},{2,18},{3,19},{4,20},{5,21},{6,22},{7,23}} | collective-permute-start | bytes 1769480 | tf_op jit(solution)/shard_map/ppermute | solution.py:465
  253.1 4.8 %turn.1.refs_0_ = bf16[1536,768]{1,0:T(8,128)(2,1)} custom-call(s32[2]{0:T(128)} %pad_add_fusion.place, bf16[3,192,1536]{2,1,0:T(8,128)(2,1)} %get-tuple-element.37.refs_0_, bf16[768,1536]{1,0:T(8,128)(2,1)} %first_mix.1.refs_9_.refs_1_, bf16[192,1536]{1,0:T(8,128)(2,1)} %copy-done.19, bf16[192,1536]{1,0:T(8,128)(2,1)} %copy-done.18, ...), custom_call_target="tpu_custom_call" | custom-call | bytes 4718592 | tf_op jit(solution)/shard_map/turn/pallas_call | solution.py:396
  258.0 4.9 %collective-permute-done.36.refs_12_ = bf16[192,1536]{1,0:T(8,128)(2,1)S(1)} collective-permute-done((bf16[192,1536]{1,0:T(8,128)(2,1)S(1)}, bf16[192,1536]{1,0:T(8,128)(2,1)S(1)}, u32[]{:S(2)}, u32[]{:S(2)}) %collective-permute-start.36) | collective-permute-done | bytes 589856 | tf_op jit(solution)/shard_map/ppermute | solution.py:465
  262.9 0.8 copy-done.11
  263.7 0.8 copy-done.12
  264.5 7.2 %term.2 = bf16[4,192,1536]{2,1,0:T(8,128)(2,1)} custom-call(s32[2]{0:T(128)} %pad_add_fusion.place, bf16[1536,768]{1,0:T(8,128)(2,1)} %turn.1.refs_0_, bf16[768,1536]{1,0:T(8,128)(2,1)} %bitcast.52, bf16[192,1536]{1,0:T(8,128)(2,1)} %get-tuple-element.41.refs_2_, bf16[192,1536]{1,0:T(8,128)(2,1)} %copy-done.6, ...), custom_call_target="tpu_custom_call" | custom-call | flops 1811939328 | bytes 9437184 | tf_op jit(solution)/shard_map/term/pallas_call | solution.py:449
  272.6 11.3 %back.5 = f32[8,128]{1,0:T(8,128)} custom-call(s32[16]{0:T(128)} %stack.110.scalars, bf16[768,1536]{1,0:T(8,128)(2,1)} %constant_dynamic-update-slice_fusion.refs_0_, bf16[768,1536]{1,0:T(8,128)(2,1)} %copy-done, bf16[768,1536]{1,0:T(8,128)(2,1)} %constant_dynamic-update-slice_fusion.10.refs_2_, ...), custom_call_target="tpu_custom_call" | custom-call | flops 3623878656 | bytes 7077888 | tf_op jit(solution)/shard_map/back/pallas_call | solution.py:344
  284.6 1.4 copy-done.2
  286.0 7.9 %term.3 = bf16[4,192,1536]{2,1,0:T(8,128)(2,1)} custom-call(s32[2]{0:T(128)} %pad_add_fusion.place, bf16[1536,768]{1,0:T(8,128)(2,1)} %turn.1.refs_0_, bf16[768,1536]{1,0:T(8,128)(2,1)} %bitcast.53, bf16[192,1536]{1,0:T(8,128)(2,1)} %get-tuple-element.41.refs_2_, bf16[192,1536]{1,0:T(8,128)(2,1)} %copy-done.6, ...), custom_call_target="tpu_custom_call" | custom-call | flops 1811939328 | bytes 9437184 | tf_op jit(solution)/shard_map/term/pallas_call | solution.py:449
  294.0 1.5 dynamic-slice_bitcast_fusion.2
  295.5 2.4 collective-permute-start.39
  297.9 2.4 collective-permute-start.41
  301.9 71.8 %psum.7 = f32[4,2,128]{2,1,0:T(2,128)S(1)} all-reduce(f32[4,2,128]{2,1,0:T(2,128)S(1)} %pad_maximum_fusion), channel_id=1, replica_groups=mesh['pipe'=4,'dp'=8] {'pipe','dp'}, use_global_device_ids=true, to_apply=%region_0.1 | all-reduce | flops 1024 | bytes 8192 | tf_op jit(solution)/shard_map/psum | solution.py:588
  374.4 2.4 fusion.2
  (152 shorter events, 20.2 us)
Async XLA Ops:
  0.6 16.6 %collective-permute-start.3 = (bf16[192,1536]{1,0:T(8,128)(2,1)}, bf16[192,1536]{1,0:T(8,128)(2,1)S(1)}, u32[]{:S(2)}, u32[]{:S(2)}) collective-permute-start(bf16[192,1536]{1,0:T(8,128)(2,1)} %bitcast.57), channel_id=1, source_target_pairs={{0,16},{8,24},{16,0},{24,8},{1,17},{9,25},{17,1},{25,9},{2,18},{10... | collective-permute-start | bytes 1769480 | tf_op jit(solution)/shard_map/ppermute | solution.py:461
  3.7 15.0 %collective-permute-start.2 = (bf16[192,1536]{1,0:T(8,128)(2,1)}, bf16[192,1536]{1,0:T(8,128)(2,1)S(1)}, u32[]{:S(2)}, u32[]{:S(2)}) collective-permute-start(bf16[192,1536]{1,0:T(8,128)(2,1)} %bitcast.58), channel_id=1, source_target_pairs={{0,8},{8,0},{16,24},{24,16},{1,9},{9,1},{17,25},{25,17},{2,10},{10... | collective-permute-start | bytes 1769480 | tf_op jit(solution)/shard_map/ppermute | solution.py:461
  5.2 16.6 %collective-permute-start.1 = (bf16[192,1536]{1,0:T(8,128)(2,1)}, bf16[192,1536]{1,0:T(8,128)(2,1)S(1)}, u32[]{:S(2)}, u32[]{:S(2)}) collective-permute-start(bf16[192,1536]{1,0:T(8,128)(2,1)} %bitcast.59), channel_id=1, source_target_pairs={{2,0},{3,1},{4,2},{5,3},{6,4},{7,5},{10,8},{11,9},{12,10},{13,11},... | collective-permute-start | bytes 1769480 | tf_op jit(solution)/shard_map/ppermute | solution.py:506
  6.4 16.6 %collective-permute-start = (bf16[192,1536]{1,0:T(8,128)(2,1)}, bf16[192,1536]{1,0:T(8,128)(2,1)S(1)}, u32[]{:S(2)}, u32[]{:S(2)}) collective-permute-start(bf16[192,1536]{1,0:T(8,128)(2,1)} %bitcast.60), channel_id=1, source_target_pairs={{0,2},{1,3},{2,4},{3,5},{4,6},{5,7},{8,10},{9,11},{10,12},{11,13},... | collective-permute-start | bytes 1769480 | tf_op jit(solution)/shard_map/ppermute | solution.py:505
  17.2 10.8 %copy-start.13 = (bf16[192,1536]{1,0:T(8,128)(2,1)}, bf16[192,1536]{1,0:T(8,128)(2,1)S(1)}, u32[]{:S(2)}) copy-start(bf16[192,1536]{1,0:T(8,128)(2,1)S(1)} %collective-permute-done.3) | copy-start | bytes 1769476
  18.7 9.3 %copy-start.15 = (bf16[192,1536]{1,0:T(8,128)(2,1)}, bf16[192,1536]{1,0:T(8,128)(2,1)S(1)}, u32[]{:S(2)}) copy-start(bf16[192,1536]{1,0:T(8,128)(2,1)S(1)} %collective-permute-done.2) | copy-start | bytes 1769476
  23.1 9.4 %collective-permute-start.4 = (bf16[96,1536]{1,0:T(8,128)(2,1)S(1)}, bf16[96,1536]{1,0:T(8,128)(2,1)S(1)}, u32[]{:S(2)}, u32[]{:S(2)}) collective-permute-start(bf16[96,1536]{1,0:T(8,128)(2,1)S(1)} %slice.60), channel_id=1, source_target_pairs={{0,16},{8,24},{16,0},{24,8},{1,17},{9,25},{17,1},{25,9},{2,18},{10... | collective-permute-start | bytes 884744 | tf_op jit(solution)/shard_map/ppermute | solution.py:461
  23.6 26.9 %collective-permute-start.6 = (bf16[192,1536]{1,0:T(8,128)(2,1)S(1)}, bf16[192,1536]{1,0:T(8,128)(2,1)S(1)}, u32[]{:S(2)}, u32[]{:S(2)}) collective-permute-start(bf16[192,1536]{1,0:T(8,128)(2,1)S(1)} %collective-permute-done), channel_id=1, source_target_pairs={{0,2},{1,3},{2,4},{3,5},{4,6},{5,7},{8,10},{9,11},{10,12},{11,13},... | collective-permute-start | bytes 1769480 | tf_op jit(solution)/shard_map/ppermute | solution.py:505
  28.0 22.6 %collective-permute-start.7 = (bf16[192,1536]{1,0:T(8,128)(2,1)S(1)}, bf16[192,1536]{1,0:T(8,128)(2,1)S(1)}, u32[]{:S(2)}, u32[]{:S(2)}) collective-permute-start(bf16[192,1536]{1,0:T(8,128)(2,1)S(1)} %collective-permute-done.1), channel_id=1, source_target_pairs={{2,0},{3,1},{4,2},{5,3},{6,4},{7,5},{10,8},{11,9},{12,10},{13,11},... | collective-permute-start | bytes 1769480 | tf_op jit(solution)/shard_map/ppermute | solution.py:506
  29.4 21.1 %collective-permute-start.9 = (bf16[192,1536]{1,0:T(8,128)(2,1)S(1)}, bf16[192,1536]{1,0:T(8,128)(2,1)S(1)}, u32[]{:S(2)}, u32[]{:S(2)}) collective-permute-start(bf16[192,1536]{1,0:T(8,128)(2,1)S(1)} %get-tuple-element.53), channel_id=1, source_target_pairs={{0,16},{8,24},{16,0},{24,8},{1,17},{9,25},{17,1},{25,9},{2,18},{10... | collective-permute-start | bytes 1769480 | tf_op jit(solution)/shard_map/ppermute | solution.py:461
  31.0 19.5 %collective-permute-start.8 = (bf16[192,1536]{1,0:T(8,128)(2,1)S(1)}, bf16[192,1536]{1,0:T(8,128)(2,1)S(1)}, u32[]{:S(2)}, u32[]{:S(2)}) collective-permute-start(bf16[192,1536]{1,0:T(8,128)(2,1)S(1)} %get-tuple-element.53), channel_id=1, source_target_pairs={{0,8},{8,0},{16,24},{24,16},{1,9},{9,1},{17,25},{25,17},{2,10},{10... | collective-permute-start | bytes 1769480 | tf_op jit(solution)/shard_map/ppermute | solution.py:461
  32.5 17.3 %collective-permute-start.5 = (bf16[96,1536]{1,0:T(8,128)(2,1)S(1)}, bf16[96,1536]{1,0:T(8,128)(2,1)S(1)}, u32[]{:S(2)}, u32[]{:S(2)}) collective-permute-start(bf16[96,1536]{1,0:T(8,128)(2,1)S(1)} %slice.61), channel_id=1, source_target_pairs={{0,8},{8,0},{16,24},{24,16},{1,9},{9,1},{17,25},{25,17},{2,10},{10... | collective-permute-start | bytes 884744 | tf_op jit(solution)/shard_map/ppermute | solution.py:461
  50.6 9.4 %collective-permute-start.10 = (bf16[96,1536]{1,0:T(8,128)(2,1)S(1)}, bf16[96,1536]{1,0:T(8,128)(2,1)S(1)}, u32[]{:S(2)}, u32[]{:S(2)}) collective-permute-start(bf16[96,1536]{1,0:T(8,128)(2,1)S(1)} %slice.62), channel_id=1, source_target_pairs={{0,16},{8,24},{16,0},{24,8},{1,17},{9,25},{17,1},{25,9},{2,18},{10... | collective-permute-start | bytes 884744 | tf_op jit(solution)/shard_map/ppermute | solution.py:461
  51.2 25.0 %collective-permute-start.12 = (bf16[192,1536]{1,0:T(8,128)(2,1)S(1)}, bf16[192,1536]{1,0:T(8,128)(2,1)S(1)}, u32[]{:S(2)}, u32[]{:S(2)}) collective-permute-start(bf16[192,1536]{1,0:T(8,128)(2,1)S(1)} %collective-permute-done.6), channel_id=1, source_target_pairs={{0,2},{1,3},{2,4},{3,5},{4,6},{5,7},{8,10},{9,11},{10,12},{11,13},... | collective-permute-start | bytes 1769480 | tf_op jit(solution)/shard_map/ppermute | solution.py:505
  55.5 20.7 %collective-permute-start.13 = (bf16[192,1536]{1,0:T(8,128)(2,1)S(1)}, bf16[192,1536]{1,0:T(8,128)(2,1)S(1)}, u32[]{:S(2)}, u32[]{:S(2)}) collective-permute-start(bf16[192,1536]{1,0:T(8,128)(2,1)S(1)} %collective-permute-done.7), channel_id=1, source_target_pairs={{2,0},{3,1},{4,2},{5,3},{6,4},{7,5},{10,8},{11,9},{12,10},{13,11},... | collective-permute-start | bytes 1769480 | tf_op jit(solution)/shard_map/ppermute | solution.py:506
  57.9 18.3 %collective-permute-start.15 = (bf16[192,1536]{1,0:T(8,128)(2,1)S(1)}, bf16[192,1536]{1,0:T(8,128)(2,1)S(1)}, u32[]{:S(2)}, u32[]{:S(2)}) collective-permute-start(bf16[192,1536]{1,0:T(8,128)(2,1)S(1)} %get-tuple-element.51), channel_id=1, source_target_pairs={{0,16},{8,24},{16,0},{24,8},{1,17},{9,25},{17,1},{25,9},{2,18},{10... | collective-permute-start | bytes 1769480 | tf_op jit(solution)/shard_map/ppermute | solution.py:461
  59.4 16.8 %collective-permute-start.14 = (bf16[192,1536]{1,0:T(8,128)(2,1)S(1)}, bf16[192,1536]{1,0:T(8,128)(2,1)S(1)}, u32[]{:S(2)}, u32[]{:S(2)}) collective-permute-start(bf16[192,1536]{1,0:T(8,128)(2,1)S(1)} %get-tuple-element.51), channel_id=1, source_target_pairs={{0,8},{8,0},{16,24},{24,16},{1,9},{9,1},{17,25},{25,17},{2,10},{10... | collective-permute-start | bytes 1769480 | tf_op jit(solution)/shard_map/ppermute | solution.py:461
  60.0 16.1 %collective-permute-start.11 = (bf16[96,1536]{1,0:T(8,128)(2,1)S(1)}, bf16[96,1536]{1,0:T(8,128)(2,1)S(1)}, u32[]{:S(2)}, u32[]{:S(2)}) collective-permute-start(bf16[96,1536]{1,0:T(8,128)(2,1)S(1)} %slice.63), channel_id=1, source_target_pairs={{0,8},{8,0},{16,24},{24,16},{1,9},{9,1},{17,25},{25,17},{2,10},{10... | collective-permute-start | bytes 884744 | tf_op jit(solution)/shard_map/ppermute | solution.py:461
  76.1 64.0 %collective-permute-start.22 = (bf16[768,1536]{1,0:T(8,128)(2,1)}, bf16[768,1536]{1,0:T(8,128)(2,1)}, u32[]{:S(2)}, u32[]{:S(2)}) collective-permute-start(bf16[768,1536]{1,0:T(8,128)(2,1)} %constant_dynamic-update-slice_fusion.refs_0_), channel_id=1, source_target_pairs={{0,1},{1,0},{2,3},{3,2},{4,5},{5,4},{6,7},{7,6},{8,9},{9,8},{10,11... | collective-permute-start | bytes 7077896 | tf_op jit(solution)/shard_map/ppermute | solution.py:473
  76.2 23.5 %copy-start = (bf16[768,1536]{1,0:T(8,128)(2,1)}, bf16[768,1536]{1,0:T(8,128)(2,1)S(1)}, u32[]{:S(2)}) copy-start(bf16[768,1536]{1,0:T(8,128)(2,1)S(1)} %constant_dynamic-update-slice_fusion.5.refs_1_) | copy-start | bytes 7077892
  77.6 24.2 %collective-permute-start.19 = (bf16[192,1536]{1,0:T(8,128)(2,1)S(1)}, bf16[192,1536]{1,0:T(8,128)(2,1)S(1)}, u32[]{:S(2)}, u32[]{:S(2)}) collective-permute-start(bf16[192,1536]{1,0:T(8,128)(2,1)S(1)} %get-tuple-element.49), channel_id=1, source_target_pairs={{0,16},{8,24},{16,0},{24,8},{1,17},{9,25},{17,1},{25,9},{2,18},{10... | collective-permute-start | bytes 1769480 | tf_op jit(solution)/shard_map/ppermute | solution.py:461
  78.2 24.4 %collective-permute-start.18 = (bf16[192,1536]{1,0:T(8,128)(2,1)S(1)}, bf16[192,1536]{1,0:T(8,128)(2,1)S(1)}, u32[]{:S(2)}, u32[]{:S(2)}) collective-permute-start(bf16[192,1536]{1,0:T(8,128)(2,1)S(1)} %get-tuple-element.49), channel_id=1, source_target_pairs={{0,8},{8,0},{16,24},{24,16},{1,9},{9,1},{17,25},{25,17},{2,10},{10... | collective-permute-start | bytes 1769480 | tf_op jit(solution)/shard_map/ppermute | solution.py:461
  79.1 20.6 %collective-permute-start.16 = (bf16[96,1536]{1,0:T(8,128)(2,1)S(1)}, bf16[96,1536]{1,0:T(8,128)(2,1)S(1)}, u32[]{:S(2)}, u32[]{:S(2)}) collective-permute-start(bf16[96,1536]{1,0:T(8,128)(2,1)S(1)} %slice.64), channel_id=1, source_target_pairs={{0,16},{8,24},{16,0},{24,8},{1,17},{9,25},{17,1},{25,9},{2,18},{10... | collective-permute-start | bytes 884744 | tf_op jit(solution)/shard_map/ppermute | solution.py:461
  81.2 19.3 %collective-permute-start.17 = (bf16[96,1536]{1,0:T(8,128)(2,1)S(1)}, bf16[96,1536]{1,0:T(8,128)(2,1)S(1)}, u32[]{:S(2)}, u32[]{:S(2)}) collective-permute-start(bf16[96,1536]{1,0:T(8,128)(2,1)S(1)} %slice.65), channel_id=1, source_target_pairs={{0,8},{8,0},{16,24},{24,16},{1,9},{9,1},{17,25},{25,17},{2,10},{10... | collective-permute-start | bytes 884744 | tf_op jit(solution)/shard_map/ppermute | solution.py:461
  99.7 40.5 %collective-permute-start.23 = (bf16[768,1536]{1,0:T(8,128)(2,1)S(1)}, bf16[768,1536]{1,0:T(8,128)(2,1)}, u32[]{:S(2)}, u32[]{:S(2)}) collective-permute-start(bf16[768,1536]{1,0:T(8,128)(2,1)S(1)} %constant_dynamic-update-slice_fusion.5.refs_1_), channel_id=1, source_target_pairs={{0,1},{1,0},{2,3},{3,2},{4,5},{5,4},{6,7},{7,6},{8,9},{9,8},{10,11... | collective-permute-start | bytes 7077896 | tf_op jit(solution)/shard_map/ppermute | solution.py:473
  101.2 11.5 %copy-start.29 = (s32[4]{0:T(128)S(1)}, s32[4]{0:T(128)}, u32[]{:S(2)}) copy-start(s32[4]{0:T(128)} %constant.112.clone) | copy-start | bytes 52
  101.2 12.8 %copy-start.28 = (s32[4]{0:T(128)S(1)}, s32[4]{0:T(128)}, u32[]{:S(2)}) copy-start(s32[4]{0:T(128)} %constant.111.clone) | copy-start | bytes 52
  101.2 14.0 %copy-start.27 = (s32[4]{0:T(128)S(1)}, s32[4]{0:T(128)}, u32[]{:S(2)}) copy-start(s32[4]{0:T(128)} %constant.110.clone) | copy-start | bytes 52
  101.2 15.3 %copy-start.26 = (bf16[1,2,128]{2,1,0:T(2,128)(2,1)S(1)}, bf16[1,2,128]{2,1,0:T(2,128)(2,1)}, u32[]{:S(2)}) copy-start(bf16[1,2,128]{2,1,0:T(2,128)(2,1)} %param.18) | copy-start | bytes 1540
  101.2 38.9 %collective-permute-start.24 = (bf16[768,1536]{1,0:T(8,128)(2,1)}, bf16[768,1536]{1,0:T(8,128)(2,1)}, u32[]{:S(2)}, u32[]{:S(2)}) collective-permute-start(bf16[768,1536]{1,0:T(8,128)(2,1)} %constant_dynamic-update-slice_fusion.10.refs_2_), channel_id=1, source_target_pairs={{0,1},{1,0},{2,3},{3,2},{4,5},{5,4},{6,7},{7,6},{8,9},{9,8},{10,11... | collective-permute-start | bytes 7077896 | tf_op jit(solution)/shard_map/ppermute | solution.py:473
  101.8 23.3 %copy-start.20 = (s32[3,2,3,128]{3,1,2,0:T(2,128)S(1)}, s32[3,2,3,128]{3,1,2,0:T(2,128)}, u32[]{:S(2)}) copy-start(s32[3,2,3,128]{3,1,2,0:T(2,128)} %param.16) | copy-start | bytes 27652
  101.8 23.4 %copy-start.21 = (s32[128]{0:T(128)S(1)}, s32[128]{0:T(128)}, u32[]{:S(2)}) copy-start(s32[128]{0:T(128)} %constant.117.clone) | copy-start | bytes 1540
  101.9 25.6 %copy-start.22 = (f32[128]{0:T(128)S(1)}, f32[128]{0:T(128)}, u32[]{:S(2)}) copy-start(f32[128]{0:T(128)} %constant.116.clone) | copy-start | bytes 1540
  101.9 25.6 %copy-start.23 = (f32[128]{0:T(128)S(1)}, f32[128]{0:T(128)}, u32[]{:S(2)}) copy-start(f32[128]{0:T(128)} %constant.115.clone) | copy-start | bytes 1540
  101.9 25.6 %copy-start.24 = (pred[128]{0:T(512)(128)(4,1)S(1)}, pred[128]{0:T(512)(128)(4,1)}, u32[]{:S(2)}) copy-start(pred[128]{0:T(512)(128)(4,1)} %constant.114.clone) | copy-start | bytes 388
  101.9 25.6 %copy-start.25 = (pred[128]{0:T(512)(128)(4,1)S(1)}, pred[128]{0:T(512)(128)(4,1)}, u32[]{:S(2)}) copy-start(pred[128]{0:T(512)(128)(4,1)} %constant.113.clone) | copy-start | bytes 388
  101.9 10.1 %collective-permute-start.21 = (bf16[96,1536]{1,0:T(8,128)(2,1)S(1)}, bf16[96,1536]{1,0:T(8,128)(2,1)S(1)}, u32[]{:S(2)}, u32[]{:S(2)}) collective-permute-start(bf16[96,1536]{1,0:T(8,128)(2,1)S(1)} %slice.82), channel_id=1, source_target_pairs={{0,8},{8,0},{16,24},{24,16},{1,9},{9,1},{17,25},{25,17},{2,10},{10... | collective-permute-start | bytes 884744 | tf_op jit(solution)/shard_map/ppermute | solution.py:461
  102.5 8.7 %collective-permute-start.20 = (bf16[96,1536]{1,0:T(8,128)(2,1)S(1)}, bf16[96,1536]{1,0:T(8,128)(2,1)S(1)}, u32[]{:S(2)}, u32[]{:S(2)}) collective-permute-start(bf16[96,1536]{1,0:T(8,128)(2,1)S(1)} %slice.81), channel_id=1, source_target_pairs={{0,16},{8,24},{16,0},{24,8},{1,17},{9,25},{17,1},{25,9},{2,18},{10... | collective-permute-start | bytes 884744 | tf_op jit(solution)/shard_map/ppermute | solution.py:461
  112.8 27.4 %collective-permute-start.25 = (bf16[768,1536]{1,0:T(8,128)(2,1)}, bf16[768,1536]{1,0:T(8,128)(2,1)}, u32[]{:S(2)}, u32[]{:S(2)}) collective-permute-start(bf16[768,1536]{1,0:T(8,128)(2,1)} %constant_dynamic-update-slice_fusion.15.refs_3_), channel_id=1, source_target_pairs={{0,1},{1,0},{2,3},{3,2},{4,5},{5,4},{6,7},{7,6},{8,9},{9,8},{10,11... | collective-permute-start | bytes 7077896 | tf_op jit(solution)/shard_map/ppermute | solution.py:473
  180.8 17.1 %copy-start.4 = (bf16[192,1536]{1,0:T(8,128)(2,1)S(1)}, bf16[192,1536]{1,0:T(8,128)(2,1)}, u32[]{:S(2)}) copy-start(bf16[192,1536]{1,0:T(8,128)(2,1)} %get-tuple-element.42.refs_6_) | copy-start | bytes 1769476
  180.8 17.8 %copy-start.1 = (bf16[3,192,1536]{2,1,0:T(8,128)(2,1)S(1)}, bf16[3,192,1536]{2,1,0:T(8,128)(2,1)}, u32[]{:S(2)}) copy-start(bf16[3,192,1536]{2,1,0:T(8,128)(2,1)} %get-tuple-element.37.refs_0_) | copy-start | bytes 5308420
  193.8 33.0 %copy-start.3 = (bf16[192,1536]{1,0:T(8,128)(2,1)S(1)}, bf16[192,1536]{1,0:T(8,128)(2,1)}, u32[]{:S(2)}) copy-start(bf16[192,1536]{1,0:T(8,128)(2,1)} %get-tuple-element.43.refs_10_) | copy-start | bytes 1769476
  193.8 17.0 %collective-permute-start.31 = (bf16[192,1536]{1,0:T(8,128)(2,1)}, bf16[192,1536]{1,0:T(8,128)(2,1)S(1)}, u32[]{:S(2)}, u32[]{:S(2)}) collective-permute-start(bf16[192,1536]{1,0:T(8,128)(2,1)} %get-tuple-element.41.refs_2_), channel_id=1, source_target_pairs={{24,0},{25,1},{26,2},{27,3},{28,4},{29,5},{30,6},{31,7}} | collective-permute-start | bytes 1769480 | tf_op jit(solution)/shard_map/ppermute | solution.py:465
  195.2 28.2 %collective-permute-start.30 = (bf16[192,1536]{1,0:T(8,128)(2,1)}, bf16[192,1536]{1,0:T(8,128)(2,1)}, u32[]{:S(2)}, u32[]{:S(2)}) collective-permute-start(bf16[192,1536]{1,0:T(8,128)(2,1)} %get-tuple-element.41.refs_2_), channel_id=1, source_target_pairs={{16,0},{17,1},{18,2},{19,3},{20,4},{21,5},{22,6},{23,7}} | collective-permute-start | bytes 1769480 | tf_op jit(solution)/shard_map/ppermute | solution.py:465
  196.5 28.2 %collective-permute-start.29 = (bf16[192,1536]{1,0:T(8,128)(2,1)}, bf16[192,1536]{1,0:T(8,128)(2,1)S(1)}, u32[]{:S(2)}, u32[]{:S(2)}) collective-permute-start(bf16[192,1536]{1,0:T(8,128)(2,1)} %get-tuple-element.41.refs_2_), channel_id=1, source_target_pairs={{8,0},{9,1},{10,2},{11,3},{12,4},{13,5},{14,6},{15,7}} | collective-permute-start | bytes 1769480 | tf_op jit(solution)/shard_map/ppermute | solution.py:465
  197.8 27.6 %collective-permute-start.34 = (bf16[192,1536]{1,0:T(8,128)(2,1)S(1)}, bf16[192,1536]{1,0:T(8,128)(2,1)S(1)}, u32[]{:S(2)}, u32[]{:S(2)}) collective-permute-start(bf16[192,1536]{1,0:T(8,128)(2,1)S(1)} %copy-done.4), channel_id=1, source_target_pairs={{16,8},{17,9},{18,10},{19,11},{20,12},{21,13},{22,14},{23,15}} | collective-permute-start | bytes 1769480 | tf_op jit(solution)/shard_map/ppermute | solution.py:465
  198.7 28.1 %collective-permute-start.28 = (bf16[192,1536]{1,0:T(8,128)(2,1)S(1)}, bf16[192,1536]{1,0:T(8,128)(2,1)S(1)}, u32[]{:S(2)}, u32[]{:S(2)}) collective-permute-start(bf16[192,1536]{1,0:T(8,128)(2,1)S(1)} %get-tuple-element.57), channel_id=1, source_target_pairs={{0,24},{8,16},{16,8},{1,25},{9,17},{17,9},{2,26},{10,18},{18,10},{... | collective-permute-start | bytes 1769480 | tf_op jit(solution)/shard_map/ppermute | solution.py:569
  210.7 47.1 %copy-start.5 = (bf16[192,1536]{1,0:T(8,128)(2,1)}, bf16[192,1536]{1,0:T(8,128)(2,1)S(1)}, u32[]{:S(2)}) copy-start(bf16[192,1536]{1,0:T(8,128)(2,1)S(1)} %collective-permute-done.31.refs_5_) | copy-start | bytes 1769476
  210.7 36.6 %collective-permute-start.27 = (bf16[192,1536]{1,0:T(8,128)(2,1)S(1)}, bf16[192,1536]{1,0:T(8,128)(2,1)S(1)}, u32[]{:S(2)}, u32[]{:S(2)}) collective-permute-start(bf16[192,1536]{1,0:T(8,128)(2,1)S(1)} %get-tuple-element.58), channel_id=1, source_target_pairs={{0,16},{8,24},{24,8},{1,17},{9,25},{25,9},{2,18},{10,26},{26,10},{... | collective-permute-start | bytes 1769480 | tf_op jit(solution)/shard_map/ppermute | solution.py:569
  223.4 28.3 %collective-permute-start.26 = (bf16[192,1536]{1,0:T(8,128)(2,1)S(1)}, bf16[192,1536]{1,0:T(8,128)(2,1)S(1)}, u32[]{:S(2)}, u32[]{:S(2)}) collective-permute-start(bf16[192,1536]{1,0:T(8,128)(2,1)S(1)} %get-tuple-element.59), channel_id=1, source_target_pairs={{0,8},{16,24},{24,16},{1,9},{17,25},{25,17},{2,10},{18,26},{26,18}... | collective-permute-start | bytes 1769480 | tf_op jit(solution)/shard_map/ppermute | solution.py:569
  224.7 33.2 %copy-start.6 = (bf16[192,1536]{1,0:T(8,128)(2,1)}, bf16[192,1536]{1,0:T(8,128)(2,1)S(1)}, u32[]{:S(2)}) copy-start(bf16[192,1536]{1,0:T(8,128)(2,1)S(1)} %collective-permute-done.29.refs_3_) | copy-start | bytes 1769476
  224.7 33.2 %collective-permute-start.33 = (bf16[192,1536]{1,0:T(8,128)(2,1)S(1)}, bf16[192,1536]{1,0:T(8,128)(2,1)S(1)}, u32[]{:S(2)}, u32[]{:S(2)}) collective-permute-start(bf16[192,1536]{1,0:T(8,128)(2,1)S(1)} %copy-done.4), channel_id=1, source_target_pairs={{24,8},{25,9},{26,10},{27,11},{28,12},{29,13},{30,14},{31,15}} | collective-permute-start | bytes 1769480 | tf_op jit(solution)/shard_map/ppermute | solution.py:465
  225.4 32.4 %copy-start.7 = (bf16[192,1536]{1,0:T(8,128)(2,1)}, bf16[192,1536]{1,0:T(8,128)(2,1)S(1)}, u32[]{:S(2)}) copy-start(bf16[192,1536]{1,0:T(8,128)(2,1)S(1)} %collective-permute-done.34.refs_9_) | copy-start | bytes 1769476
  225.5 32.5 %collective-permute-start.32 = (bf16[192,1536]{1,0:T(8,128)(2,1)S(1)}, bf16[192,1536]{1,0:T(8,128)(2,1)S(1)}, u32[]{:S(2)}, u32[]{:S(2)}) collective-permute-start(bf16[192,1536]{1,0:T(8,128)(2,1)S(1)} %copy-done.4), channel_id=1, source_target_pairs={{0,8},{1,9},{2,10},{3,11},{4,12},{5,13},{6,14},{7,15}} | collective-permute-start | bytes 1769480 | tf_op jit(solution)/shard_map/ppermute | solution.py:465
  226.8 26.3 %copy-start.17 = (bf16[192,1536]{1,0:T(8,128)(2,1)}, bf16[192,1536]{1,0:T(8,128)(2,1)S(1)}, u32[]{:S(2)}) copy-start(bf16[192,1536]{1,0:T(8,128)(2,1)S(1)} %collective-permute-done.28.refs_4_) | copy-start | bytes 1769476
  226.8 31.1 %collective-permute-start.37 = (bf16[192,1536]{1,0:T(8,128)(2,1)S(1)}, bf16[192,1536]{1,0:T(8,128)(2,1)S(1)}, u32[]{:S(2)}, u32[]{:S(2)}) collective-permute-start(bf16[192,1536]{1,0:T(8,128)(2,1)S(1)} %copy-done.3), channel_id=1, source_target_pairs={{8,16},{9,17},{10,18},{11,19},{12,20},{13,21},{14,22},{15,23}} | collective-permute-start | bytes 1769480 | tf_op jit(solution)/shard_map/ppermute | solution.py:465
  247.3 5.8 %copy-start.18 = (bf16[192,1536]{1,0:T(8,128)(2,1)}, bf16[192,1536]{1,0:T(8,128)(2,1)S(1)}, u32[]{:S(2)}) copy-start(bf16[192,1536]{1,0:T(8,128)(2,1)S(1)} %collective-permute-done.27.refs_3_) | copy-start | bytes 1769476
  247.3 15.6 %collective-permute-start.36 = (bf16[192,1536]{1,0:T(8,128)(2,1)S(1)}, bf16[192,1536]{1,0:T(8,128)(2,1)S(1)}, u32[]{:S(2)}, u32[]{:S(2)}) collective-permute-start(bf16[192,1536]{1,0:T(8,128)(2,1)S(1)} %copy-done.3), channel_id=1, source_target_pairs={{0,16},{1,17},{2,18},{3,19},{4,20},{5,21},{6,22},{7,23}} | collective-permute-start | bytes 1769480 | tf_op jit(solution)/shard_map/ppermute | solution.py:465
  251.7 11.2 %collective-permute-start.35 = (bf16[192,1536]{1,0:T(8,128)(2,1)S(1)}, bf16[192,1536]{1,0:T(8,128)(2,1)S(1)}, u32[]{:S(2)}, u32[]{:S(2)}) collective-permute-start(bf16[192,1536]{1,0:T(8,128)(2,1)S(1)} %copy-done.3), channel_id=1, source_target_pairs={{24,16},{25,17},{26,18},{27,19},{28,20},{29,21},{30,22},{31,23}} | collective-permute-start | bytes 1769480 | tf_op jit(solution)/shard_map/ppermute | solution.py:465
  257.9 5.0 %copy-start.8 = (bf16[192,1536]{1,0:T(8,128)(2,1)}, bf16[192,1536]{1,0:T(8,128)(2,1)S(1)}, u32[]{:S(2)}) copy-start(bf16[192,1536]{1,0:T(8,128)(2,1)S(1)} %collective-permute-done.33.refs_8_) | copy-start | bytes 1769476
  271.8 12.8 %collective-permute-start.38 = (bf16[4,192,1536]{2,1,0:T(8,128)(2,1)}, bf16[4,192,1536]{2,1,0:T(8,128)(2,1)S(1)}, u32[]{:S(2)}, u32[]{:S(2)}) collective-permute-start(bf16[4,192,1536]{2,1,0:T(8,128)(2,1)} %term.2), channel_id=1, source_target_pairs={{0,1},{1,0},{2,3},{3,2},{4,5},{5,4},{6,7},{7,6},{8,9},{9,8},{10,11... | collective-permute-start | bytes 7077896 | tf_op jit(solution)/shard_map/ppermute | solution.py:473
  295.5 78.8 %collective-permute-start.39 = (bf16[192,1536]{1,0:T(8,128)(2,1)S(1)}, bf16[192,1536]{1,0:T(8,128)(2,1)S(1)}, u32[]{:S(2)}, u32[]{:S(2)}) collective-permute-start(bf16[192,1536]{1,0:T(8,128)(2,1)S(1)} %get-tuple-element.54), channel_id=1, source_target_pairs={{0,2},{1,3},{2,0},{3,1},{4,6},{5,7},{6,4},{7,5},{8,10},{9,11},{10,... | collective-permute-start | bytes 1769480 | tf_op jit(solution)/shard_map/ppermute | solution.py:469
  297.9 76.4 %collective-permute-start.41 = (bf16[192,1536]{1,0:T(8,128)(2,1)S(1)}, bf16[192,1536]{1,0:T(8,128)(2,1)S(1)}, u32[]{:S(2)}, u32[]{:S(2)}) collective-permute-start(bf16[192,1536]{1,0:T(8,128)(2,1)S(1)} %get-tuple-element.55), channel_id=1, source_target_pairs={{0,6},{1,7},{2,4},{3,5},{4,2},{5,3},{6,0},{7,1},{8,14},{9,15},{10,... | collective-permute-start | bytes 1769480 | tf_op jit(solution)/shard_map/ppermute | solution.py:469
  300.4 74.0 %collective-permute-start.40 = (bf16[192,1536]{1,0:T(8,128)(2,1)S(1)}, bf16[192,1536]{1,0:T(8,128)(2,1)S(1)}, u32[]{:S(2)}, u32[]{:S(2)}) collective-permute-start(bf16[192,1536]{1,0:T(8,128)(2,1)S(1)} %get-tuple-element.56), channel_id=1, source_target_pairs={{0,4},{1,5},{2,6},{3,7},{4,0},{5,1},{6,2},{7,3},{8,12},{9,13},{10,... | collective-permute-start | bytes 1769480 | tf_op jit(solution)/shard_map/ppermute | solution.py:469
  (8 other events, 19.0 us)
